TPU v7x, 128 devices: a whole 4x4x4 slice. The times are simulated.
128 devices in a mesh: row: 8 (over z, core), col: 16 (over x, y).
Axes of the slice: x: 4, y: 4, z: 4, core: 2. Of those that a mesh axis runs over, the one named last changes fastest.
Arguments:
- front_matrix: float32 [16384, 16384], P('row', 'col'), may hold values from -168 to 3072, as said below
- child_blocks: float32 [1024, 256, 256], P(('row', 'col')), may hold values from -3 to 3
- child_target: int32 [1024, 2], P(('row', 'col')), may hold values from 8 to 63, as said below
- child_place: int32 [1024, 2, 256], P(('row', 'col')), may hold values from 0 to 255, as said below
- child_live: int32 [1024, 2], P(('row', 'col')), may hold values from 128 to 256
Outputs:
- factored: float32 [16384, 16384], P('row', 'col')
Inputs may be any that keep to these rules, and one draw needn't show every extreme that they name: The block of front_matrix on the first 1024 front rows and columns is symmetric positive definite, with smallest eigenvalue at least 0.3 * 2 * 2 * 256. child_target[k,0] leaves the same remainder modulo 8 as the mesh row of the device holding block k, and is at least 8; child_target[k,1] is at least 16; the blocks held by one device name at most 2 distinct blocks whose column leaves one remainder modulo 16, and in every mesh row some remainder receives 2 blocks from every device of that row. Each row child_place[k,i,:] is a permutation of 0 .. 255.
All inputs are finite; a program needn't handle non-finite values.
Results may differ from a plain program's by a relative error of at most 0.0003.
Values sent between devices are 32-bit elements; how exact they have to be, the bound alone decides.
No kernel may reach another device: no remote copies, remote signals or barrier semaphores. Data moves between devices by JAX's collectives and lax.ppermute only.
A program may use at most 128 MiB of HBM per device.

v0:
```python
import functools

import jax
import jax.numpy as jnp
from jax import lax
from jax.experimental import pallas as pl
from jax.experimental.pallas import tpu as pltpu
from jax.sharding import PartitionSpec as P

F32 = jnp.float32
BF16 = jnp.bfloat16
I32 = jnp.int32
BLK = 256
LEADS = 4
CAP = 2
SIDE = 4
NB = 128
HIGHEST = lax.Precision.HIGHEST


def dot_nt(left, right, precision=None):
    return lax.dot_general(
        left, right, (((1,), (1,)), ((), ())), precision=precision, preferred_element_type=F32
    )


def dot_nn(left, right, precision=None):
    return lax.dot_general(
        left, right, (((1,), (0,)), ((), ())), precision=precision, preferred_element_type=F32
    )


def split2(value):
    high = value.astype(BF16)
    return high, (value - high.astype(F32)).astype(BF16)


def swap_cores(value):
    return lax.ppermute(value, "row", [(r, r ^ 1) for r in range(8)])


def spread_x(parts, x):
    out = jnp.where(x == 0, parts[0], jnp.zeros_like(parts[0]))
    for q in range(1, SIDE):
        out = out + lax.ppermute(parts[q], "col", [(y, q * SIDE + y) for y in range(SIDE)])
    return out


def after(value, *earlier):
    return lax.optimization_barrier((value,) + earlier)[0]


def exchange(value, axis):
    return lax.all_to_all(value, axis, split_axis=0, concat_axis=0, tiled=True)


def to_all(value, axis):
    copies = lax.axis_size(axis)
    return exchange(jnp.broadcast_to(value[None], (copies,) + value.shape), axis)


LOWER = (((0, 0), (1, 0), (2, 0), (3, 0), (1, 1)), ((2, 1), (3, 1), (2, 2), (3, 2), (3, 3)))


def lead_share(strip, core):
    four = to_all(strip, "row")[:LEADS]
    first, second = [jnp.concatenate([four[i, j] for i, j in half], axis=0) for half in LOWER]
    return jnp.where(core == 0, first, second), four


def col_pieces(slab):
    blocks = slab.reshape(8, BLK, BLK)
    out = None
    for h in range(2):
        for q in range(2):
            pairs = []
            for r in range(8):
                for j in range(LEADS):
                    pairs.append((r * 16 + j, (2 * j + q) * 16 + r + 8 * h))
            part = jnp.stack([blocks[4 * q + h], blocks[4 * q + 2 + h]])
            part = lax.ppermute(part, ("row", "col"), pairs)
            out = part if out is None else out + part
    return out


def factor_block(a, u_ref, e_ref):
    n = a.shape[0]
    ri = lax.broadcasted_iota(I32, (n, n), 0)
    ci = lax.broadcasted_iota(I32, (n, n), 1)
    e = jnp.where(ri == ci, F32(1), F32(0))
    base = 0
    for p in range(0, n, 4):
        off = p - base
        m = a.shape[0]
        cols = [jnp.broadcast_to(a[:, p + v : p + v + 1], (m, n)) for v in range(4)]
        s = [[cols[v][off + i : off + i + 1, :] for v in range(4)] for i in range(4)]
        arow = [a[off + i : off + i + 1, :] for i in range(4)]
        erow = [e[off + i : off + i + 1, :] for i in range(4)]
        inverse = []
        for q in range(4):
            r = F32(1) / s[q][q]
            inverse.append(r)
            low = [None] * 4
            for i in range(q + 1, 4):
                low[i] = s[i][q] * r
            for i in range(q + 1, 4):
                for v in range(q + 1, i + 1):
                    s[i][v] = s[i][v] - low[i] * s[v][q]
                arow[i] = arow[i] - low[i] * arow[q]
                erow[i] = erow[i] - low[i] * erow[q]
        for q in range(4):
            scale = lax.rsqrt(s[q][q])
            u_ref[p + q : p + q + 1, :] = arow[q] * scale
            e_ref[p + q : p + q + 1, :] = erow[q] * scale
        following = p + 4
        if following >= n:
            break
        live = None
        if following % 8 == 0:
            cut = following - base
            a, e, cols = a[cut:], e[cut:], [c[cut:] for c in cols]
            base = following
        else:
            live = lax.broadcasted_iota(I32, a.shape, 0) >= following - base
        times = []
        for q in range(4):
            c = cols[q]
            for v in range(q):
                c = c - times[v] * s[q][v]
            times.append(c * inverse[q])
        da = times[0] * arow[0]
        de = times[0] * erow[0]
        for q in range(1, 4):
            da = da + times[q] * arow[q]
            de = de + times[q] * erow[q]
        if live is not None:
            da = jnp.where(live, da, F32(0))
            de = jnp.where(live, de, F32(0))
        a = a - da
        e = e - de


def factor_kernel(table, own_ref, other_ref, l_ref, high_ref, low_ref, m_ref, inv_ref, u_ref, e_ref):
    n = m_ref.shape[0]
    steps = n // NB
    strips = own_ref.shape[0]
    tall = BLK // strips

    def assemble(sources):
        def place(number, carry):
            for half, source in zip(LOWER, sources):
                for spot, (i, j) in enumerate(half):
                    row = pl.multiple_of(i * BLK + number * tall, tall)
                    m_ref[pl.ds(row, tall), j * BLK : (j + 1) * BLK] = source[
                        number, spot * tall : (spot + 1) * tall, :
                    ]
            return carry

        lax.fori_loop(0, strips, place, 0)

    @pl.when(table[0] == 0)
    def _():
        assemble((own_ref, other_ref))

    @pl.when(table[0] != 0)
    def _():
        assemble((other_ref, own_ref))

    l_ref[...] = jnp.zeros_like(l_ref)
    inv_ref[...] = jnp.zeros_like(inv_ref)
    ri = lax.broadcasted_iota(I32, (NB, NB), 0)
    ci = lax.broadcasted_iota(I32, (NB, NB), 1)

    def step(k, carry):
        at = pl.multiple_of(k * NB, NB)
        d = m_ref[pl.ds(at, NB), pl.ds(at, NB)]
        factor_block(jnp.where(ri >= ci, d, d.T), u_ref, e_ref)
        l_ref[pl.ds(at, NB), pl.ds(at, NB)] = jnp.where(ri <= ci, u_ref[...], F32(0)).T
        ik = jnp.where(ri >= ci, e_ref[...], F32(0))
        for kk in range(steps):

            @pl.when(k == kk)
            def _():
                lo, hi = kk * NB, (kk + 1) * NB
                if kk < steps - 1:
                    panel = dot_nt(m_ref[hi:, lo:hi], ik, HIGHEST)
                    l_ref[hi:, lo:hi] = panel
                    m_ref[hi:, hi:] = m_ref[hi:, hi:] - dot_nt(panel, panel, HIGHEST)
                if kk > 0:
                    inv_ref[lo:hi, :lo] = dot_nn(ik, inv_ref[lo:hi, :lo], HIGHEST)
                inv_ref[lo:hi, lo:hi] = ik
                if kk < steps - 1:
                    inv_ref[hi:, :hi] = inv_ref[hi:, :hi] - dot_nn(
                        panel, inv_ref[lo:hi, :hi], HIGHEST
                    )

        return carry

    lax.fori_loop(0, steps, step, 0)
    for i in range(LEADS):
        rows = slice(i * BLK, (i + 1) * BLK)
        high_ref[rows, :], low_ref[rows, :] = split2(inv_ref[rows, :])


def factor_lead(table, *parts):
    n = LEADS * BLK
    vmem = pl.BlockSpec(memory_space=pltpu.VMEM)
    return pl.pallas_call(
        factor_kernel,
        out_shape=(
            jax.ShapeDtypeStruct((n, n), F32),
            jax.ShapeDtypeStruct((n, n), BF16),
            jax.ShapeDtypeStruct((n, n), BF16),
        ),
        in_specs=[pl.BlockSpec(memory_space=pltpu.SMEM)] + [vmem] * 2,
        out_specs=[vmem, vmem, vmem],
        scratch_shapes=[
            pltpu.VMEM((n, n), F32),
            pltpu.VMEM((n, n), F32),
            pltpu.VMEM((NB, NB), F32),
            pltpu.VMEM((NB, NB), F32),
        ],
        compiler_params=pltpu.CompilerParams(vmem_limit_bytes=40 << 20),
        cost_estimate=pl.CostEstimate(flops=60_000_000_000, bytes_accessed=10 << 20, transcendentals=0),
        name="factor_lead",
    )(table, *parts)


def update_kernel(table, *refs):
    uc, raw = refs[0:4], refs[4:8]
    front_ref, own_ref, high_ref, low_ref, out_ref = refs[8:13]
    ch, cl, rh, rl, pan = refs[13:]
    g = pl.program_id(0)
    r, c = table[0], table[1]

    upper, lower = slice(0, BLK), slice(BLK, 2 * BLK)

    def solve():
        high, low = rh[...], rl[...]
        out = []
        for j in range(LEADS):
            hi = (j + 1) * BLK
            rows = slice(j * BLK, hi)
            out.append(
                dot_nt(high[:, :hi], high_ref[rows, :hi])
                + (
                    dot_nt(high[:, :hi], low_ref[rows, :hi])
                    + dot_nt(low[:, :hi], high_ref[rows, :hi])
                )
            )
        return out

    @pl.when(g < 2)
    def _():
        for j in range(LEADS):
            cols = slice(j * BLK, (j + 1) * BLK)
            rh[upper, cols], rl[upper, cols] = split2(uc[j][0, 0])
            rh[lower, cols], rl[lower, cols] = split2(uc[j][0, 1])
        got = solve()
        at = pl.ds(pl.multiple_of(g * 2 * BLK, BLK), 2 * BLK)
        for j in range(LEADS):
            cols = slice(j * BLK, (j + 1) * BLK)
            ch[at, cols], cl[at, cols] = split2(got[j])

    @pl.when(g >= 2)
    def _():
        for j in range(LEADS):
            cols = slice(j * BLK, (j + 1) * BLK)
            rh[:, cols], rl[:, cols] = split2(raw[j][0])
        got = solve()
        special = (g == 2) & (r < LEADS)
        top = lax.broadcasted_iota(I32, (2 * BLK, BLK), 0) < BLK
        left = []
        for j in range(LEADS):
            cols = slice(j * BLK, (j + 1) * BLK)
            own = own_ref[:, cols]
            own = jnp.concatenate([own, own], axis=0)
            keep = jnp.where((r >= 2) & (j < 2), F32(1), F32(0))
            left.append(jnp.where(top & special, own * keep, got[j]))

            @pl.when(c == j)
            def _():
                pan[...] = jnp.where(top & special, own, got[j])

        left_h, left_l = split2(jnp.concatenate(left, axis=1))
        for t in range(4):
            rows = slice(t * BLK, (t + 1) * BLK)
            right_h, right_l = ch[rows, :], cl[rows, :]
            out_ref[:, rows] = front_ref[:, rows] - (
                dot_nt(left_h, right_h) + (dot_nt(left_h, right_l) + dot_nt(left_l, right_h))
            )

        @pl.when(c < LEADS)
        def _():
            out_ref[:, :BLK] = pan[...]


def update_front(table, uc, raw, front, factor, high, low):
    n = LEADS * BLK
    rows, cols = front.shape
    tall = 2 * BLK

    def step(g):
        return jnp.maximum(g - 2, 0)

    def tall_spec():
        return pl.BlockSpec((tall, cols), lambda g, t: (step(g), 0))

    def raw_spec(j):
        return pl.BlockSpec((1, tall, BLK), lambda g, t: (step(g) * SIDE + j, 0, 0))

    def uc_spec(j):
        return pl.BlockSpec((1, 2, BLK, BLK), lambda g, t: (2 * j + jnp.minimum(g, 1), 0, 0, 0))

    in_specs = [uc_spec(j) for j in range(LEADS)]
    in_specs += [raw_spec(j) for j in range(LEADS)]
    in_specs += [
        tall_spec(),
        pl.BlockSpec((BLK, n), lambda g, t: (jnp.minimum(t[0], LEADS - 1), 0)),
        pl.BlockSpec((n, n), lambda g, t: (0, 0)),
        pl.BlockSpec((n, n), lambda g, t: (0, 0)),
    ]
    return pl.pallas_call(
        update_kernel,
        out_shape=jax.ShapeDtypeStruct((rows, cols), F32),
        grid_spec=pltpu.PrefetchScalarGridSpec(
            num_scalar_prefetch=1,
            grid=(2 + rows // tall,),
            in_specs=in_specs,
            out_specs=tall_spec(),
            scratch_shapes=[
                pltpu.VMEM((n, n), BF16),
                pltpu.VMEM((n, n), BF16),
                pltpu.VMEM((tall, n), BF16),
                pltpu.VMEM((tall, n), BF16),
                pltpu.VMEM((tall, BLK), F32),
            ],
        ),
        compiler_params=pltpu.CompilerParams(vmem_limit_bytes=58 << 20),
        cost_estimate=pl.CostEstimate(flops=26_000_000_000, bytes_accessed=36 << 20, transcendentals=0),
        name="update_front",
    )(table, *([uc] * LEADS), *([raw] * LEADS), front, factor, high, low)


def slots_of(target, mesh_cols):
    kids = target.shape[-2]
    same = jnp.all(target[..., :, None, :] == target[..., None, :, :], axis=-1)
    number = jnp.arange(kids, dtype=I32)
    first = jnp.min(jnp.where(same, number, kids), axis=-1)
    leads = first == number
    goal = target[..., 1] % mesh_cols
    alike = (goal[..., :, None] == goal[..., None, :]) & leads[..., None, :]
    rank = jnp.sum((alike & (number < first[..., :, None])).astype(I32), axis=-1)
    return goal * CAP + rank, leads


def sort_order(keys):
    count = keys.shape[0]
    number = jnp.arange(count, dtype=I32)
    before = (keys[None, :] < keys[:, None]) | (
        (keys[None, :] == keys[:, None]) & (number[None, :] < number[:, None])
    )
    place = jnp.sum(before.astype(I32), axis=1)
    hot = (place[None, :] == number[:, None]).astype(I32)
    return lambda values: jnp.sum(hot * values[None, :], axis=1)


def map_kernel(table, block_ref, place_ref, out_ref):
    k = pl.program_id(0)
    live_row, live_col = table[16 + k], table[24 + k]
    target = lax.broadcasted_iota(I32, (BLK, BLK), 0)
    source = lax.broadcasted_iota(I32, (BLK, BLK), 1)

    def picks(index, live):
        hit = (place_ref[0, index : index + 1, :] == target) & (source < live)
        return jnp.where(hit, F32(1), F32(0)).astype(BF16)

    def parts(value):
        high = value.astype(BF16)
        rest = value - high.astype(F32)
        middle = rest.astype(BF16)
        return high, middle, (rest - middle.astype(F32)).astype(BF16)

    row_pick, col_pick = picks(0, live_row), picks(1, live_col)
    high, middle, low = parts(block_ref[0])
    moved = dot_nn(row_pick, high) + (dot_nn(row_pick, middle) + dot_nn(row_pick, low))
    high, middle, low = parts(moved)
    mapped = dot_nt(high, col_pick) + (dot_nt(middle, col_pick) + dot_nt(low, col_pick))
    opens = (k == 0) | (table[8 + k] != table[8 + jnp.maximum(k - 1, 0)])

    @pl.when(opens)
    def _():
        out_ref[0] = mapped

    @pl.when(jnp.logical_not(opens))
    def _():
        out_ref[0] = out_ref[0] + mapped


def map_children(child_blocks, child_target, child_place, child_live, mesh_cols):
    kids = child_blocks.shape[0]
    slot, _ = slots_of(child_target, mesh_cols)
    ordered = sort_order(slot)
    table = jnp.concatenate(
        [
            ordered(jnp.arange(kids, dtype=I32)),
            ordered(slot),
            ordered(child_live[:, 0]),
            ordered(child_live[:, 1]),
        ]
    )
    return pl.pallas_call(
        map_kernel,
        out_shape=jax.ShapeDtypeStruct((mesh_cols * CAP, BLK, BLK), F32),
        grid_spec=pltpu.PrefetchScalarGridSpec(
            num_scalar_prefetch=1,
            grid=(kids,),
            in_specs=[
                pl.BlockSpec((1, BLK, BLK), lambda k, t: (t[k], 0, 0)),
                pl.BlockSpec((1, 2, BLK), lambda k, t: (t[k], 0, 0)),
            ],
            out_specs=pl.BlockSpec((1, BLK, BLK), lambda k, t: (t[8 + k], 0, 0)),
        ),
        cost_estimate=pl.CostEstimate(flops=2_000_000_000, bytes_accessed=4 << 20, transcendentals=0),
        name="map_children",
    )(table, child_blocks, child_place)


def add_kernel(table, base_ref, slot_ref, out_ref, buffers, sems, next_ref):
    row = pl.program_id(0)
    total = 32
    count = table[2 * total]
    deep = buffers.shape[0]

    def copy(n):
        k = lax.rem(n, deep)
        return pltpu.make_async_copy(slot_ref.at[table[total + n]], buffers.at[k], sems.at[k])

    @pl.when(row == 0)
    def _():
        next_ref[0] = 0
        for n in range(deep):

            @pl.when(n < count)
            def _():
                copy(jnp.int32(n)).start()

    out_ref[...] = base_ref[...]

    def here(n):
        return (n < count) & (lax.div(table[jnp.minimum(n, total - 1)], 4) == row)

    def add(n):
        copy(n).wait()
        cols = pl.ds(pl.multiple_of(lax.rem(table[n], 4) * BLK, BLK), BLK)
        out_ref[:, cols] = out_ref[:, cols] + buffers[lax.rem(n, deep)]

        @pl.when(n + deep < count)
        def _():
            copy(n + deep).start()

        return n + 1

    next_ref[0] = lax.while_loop(here, add, next_ref[0])


def add_table_kernel(mesh_rows, mesh_cols, kids, info_ref, notes_ref, out_ref, head, link):
    total = mesh_cols * CAP
    column = info_ref[0]

    def clear(n, carry):
        head[n] = -1
        return carry

    lax.fori_loop(0, 32, clear, 0)

    def source(s, carry):

        def child(k, found):
            count, old, seen = found
            down, across = notes_ref[s, 2 * k], notes_ref[s, 2 * k + 1]
            tile = lax.div(down, mesh_rows) * 4 + lax.div(across, mesh_cols)
            fresh = (lax.rem(across, mesh_cols) == column) & (tile != old) & (tile != seen)

            @pl.when(fresh)
            def _():
                link[s * CAP + count] = head[tile]
                head[tile] = s * CAP + count

            return (
                jnp.where(fresh, count + 1, count),
                jnp.where(fresh, seen, old),
                jnp.where(fresh, tile, seen),
            )

        lax.fori_loop(0, kids, child, (jnp.int32(0), jnp.int32(-1), jnp.int32(-1)))
        return carry

    lax.fori_loop(0, mesh_cols, source, 0)

    def walk(tile, n):
        def one(state):
            n, slot = state
            out_ref[n] = tile
            out_ref[total + n] = slot
            return n + 1, link[slot]

        return lax.while_loop(lambda state: state[1] >= 0, one, (n, head[tile]))[0]

    count = lax.fori_loop(0, 32, walk, jnp.int32(0))
    out_ref[2 * total] = count

    def fill(n, carry):
        last = jnp.maximum(count - 1, 0)
        none = count == 0
        out_ref[n] = jnp.where(none, 0, out_ref[last])
        out_ref[total + n] = jnp.where(none, 0, out_ref[total + last])
        return carry

    lax.fori_loop(count, total, fill, 0)


def add_table(info, notes, mesh_rows, mesh_cols, kids):
    smem = pl.BlockSpec(memory_space=pltpu.SMEM)
    total = mesh_cols * CAP
    return pl.pallas_call(
        functools.partial(add_table_kernel, mesh_rows, mesh_cols, kids),
        out_shape=jax.ShapeDtypeStruct((2 * total + 1,), I32),
        in_specs=[smem, smem],
        out_specs=smem,
        scratch_shapes=[pltpu.SMEM((32,), I32), pltpu.SMEM((total,), I32)],
        name="add_table",
    )(info, notes)


def add_children(table, base, arrived):
    rows, cols = base.shape
    deep = 8

    def row_spec():
        return pl.BlockSpec((BLK, cols), lambda n, t: (n, 0))

    return pl.pallas_call(
        add_kernel,
        out_shape=jax.ShapeDtypeStruct(base.shape, F32),
        grid_spec=pltpu.PrefetchScalarGridSpec(
            num_scalar_prefetch=1,
            grid=(rows // BLK,),
            in_specs=[row_spec(), pl.BlockSpec(memory_space=pl.ANY)],
            out_specs=row_spec(),
            scratch_shapes=[
                pltpu.VMEM((deep, BLK, BLK), F32),
                pltpu.SemaphoreType.DMA((deep,)),
                pltpu.SMEM((1,), I32),
            ],
        ),
        input_output_aliases={1: 0},
        compiler_params=pltpu.CompilerParams(vmem_limit_bytes=32 << 20),
        cost_estimate=pl.CostEstimate(flops=4_000_000, bytes_accessed=24 << 20, transcendentals=0),
        name="add_children",
    )(table, base, arrived)


def on_device(front_matrix, child_blocks, child_target, child_place, child_live):
    mesh_rows = lax.axis_size("row")
    mesh_cols = lax.axis_size("col")
    row = lax.axis_index("row")
    column = lax.axis_index("col")
    x, core = column // SIDE, row % 2
    slab = front_matrix[:, :BLK]

    table = jnp.stack([row, column]).astype(I32)

    strip = exchange(slab[:BLK].reshape(mesh_cols, -1, BLK), "col")[:LEADS]
    late = after(slab, strip)
    rows = slab.shape[0] // SIDE
    piece = spread_x([late[q * rows : (q + 1) * rows] for q in range(SIDE)], x)
    uc = col_pieces(late)
    share, four = lead_share(strip, core)
    raw = lax.all_gather(after(piece, four), "col", axis=0, tiled=False)
    packed = map_children(child_blocks, child_target, child_place, child_live, mesh_cols)

    note = jnp.zeros((8, BLK), F32)
    note = note.at[0, : child_target.size].set(child_target.reshape(-1).astype(F32))
    share, packed, uc = lax.optimization_barrier(
        (jnp.concatenate([share, note], axis=0), packed, uc)
    )
    uc = lax.all_gather(uc, "row", axis=0, tiled=False)
    own = to_all(share, "col")
    packed = after(packed, own)
    arrived = exchange(packed.reshape(mesh_cols, CAP, BLK, BLK), "col")
    arrived = arrived.reshape(mesh_cols * CAP, BLK, BLK)
    other = swap_cores(own)

    factor, high, low = factor_lead(core[None].astype(I32), own, other)
    base = update_front(table, uc, raw, front_matrix, factor, high, low)
    notes = after(own, base)[:, -8, : child_target.size].astype(I32)
    arrivals = add_table(column[None].astype(I32), notes, mesh_rows, mesh_cols, child_target.shape[0])
    return add_children(arrivals, base, arrived)


def solution(mesh):
    return jax.shard_map(
        on_device,
        mesh=mesh,
        in_specs=(
            P("row", "col"),
            P(("row", "col"), None, None),
            P(("row", "col"), None),
            P(("row", "col"), None, None),
            P(("row", "col"), None),
        ),
        out_specs=P("row", "col"),
        check_vma=False,
    )
```

profile of v0, /device:TPU:23, one launch (start us, length us, event | category | flops | bytes accessed | tf_op | source)
XLA Modules:
  0.0 346.9 jit_solution(18444541984483062719)
XLA Ops:
  6.5 1.7 slice.139
  8.2 6.6 %all-to-all-start = ((f32[16,16,256]{2,1,0:T(8,128)}), f32[16,16,256]{2,1,0:T(8,128)S(1)}, u32[]{:S(2)}, u32[]{:S(2)}) async-start(f32[16,16,256]{2,1,0:T(8,128)} %bitcast.1), calls=%async_computation | async-start | bytes 524288 | tf_op jit(solution)/shard_map/all_to_all | solution.py:54
  14.8 0.7 fusion.8
  15.5 0.7 and_select_fusion.1
  16.2 0.7 convert_element_type.23
  16.9 0.8 compare_reduce_fusion
  17.9 0.2 convert_reduce_fusion.1
  18.0 0.7 multiply_add_fusion
  18.7 0.7 fusion.6
  19.4 1.7 slice.154
  21.4 0.2 convert_reduce_fusion
  21.6 0.2 select_reduce_fusion.3
  21.7 0.6 pad_add_fusion.table
  22.3 8.8 %map_children.1 = f32[32,256,256]{2,1,0:T(8,128)} custom-call(s32[32]{0:T(128)} %pad_add_fusion.table, f32[8,256,256]{2,1,0:T(8,128)} %block_ref.1, s32[8,2,256]{2,1,0:T(2,128)} %place_ref.1), custom_call_target="tpu_custom_call" | custom-call | flops 2000000000 | bytes 4194304 | tf_op jit(solution)/shard_map/map_children/pallas_call | solution.py:412
  31.1 0.9 broadcast_in_dim.19
  31.9 6.5 %all-to-all-start.1 = ((f32[8,4,16,256]{3,2,1,0:T(8,128)}), f32[8,4,16,256]{3,2,1,0:T(8,128)S(1)}, u32[]{:S(2)}, u32[]{:S(2)}) async-start(f32[8,4,16,256]{3,2,1,0:T(8,128)} %broadcast_in_dim.19), calls=%async_computation.1 | async-start | bytes 1048576 | tf_op jit(solution)/shard_map/all_to_all | solution.py:54
  38.6 0.8 pad_maximum_fusion
  39.5 0.7 collective-permute-start
  40.1 0.8 pad_maximum_fusion.2
  41.0 1.5 collective-permute-start.2
  42.5 0.8 pad_maximum_fusion.3
  43.3 1.3 collective-permute-start.3
  44.6 0.8 pad_maximum_fusion.1
  45.4 1.5 collective-permute-start.1
  46.9 1.1 all-to-all-done.1
  48.1 25.8 %collective-permute-done.3 = f32[2,256,256]{2,1,0:T(8,128)} collective-permute-done((f32[2,256,256]{2,1,0:T(8,128)}, f32[2,256,256]{2,1,0:T(8,128)}, u32[]{:S(2)}, u32[]{:S(2)}) %collective-permute-start.3) | collective-permute-done | bytes 524320 | tf_op jit(solution)/shard_map/ppermute | solution.py:81
  73.9 2.3 add_add_fusion.1
  76.2 1.2 fusion.7
  77.4 0.7 collective-permute-start.4
  78.1 1.3 collective-permute-start.6
  79.4 1.5 collective-permute-start.5
  80.9 10.6 %collective-permute-done.6 = f32[512,256]{1,0:T(8,128)} collective-permute-done((f32[512,256]{1,0:T(8,128)}, f32[512,256]{1,0:T(8,128)}, u32[]{:S(2)}, u32[]{:S(2)}) %collective-permute-start.6) | collective-permute-done | bytes 524320 | tf_op jit(solution)/shard_map/ppermute | solution.py:45
  91.5 2.1 add_add_fusion
  93.8 35.8 %all_to_all.20.own_ref = f32[16,88,256]{2,1,0:T(8,128)S(1)} all-to-all(f32[16,88,256]{2,1,0:T(8,128)S(1)} %broadcast_in_dim.22), channel_id=1, replica_groups=mesh['row'=8,'col'=16] {'col'}, dimensions={0} | all-to-all | bytes 2883584 | tf_op jit(solution)/shard_map/all_to_all | solution.py:54
  129.6 2.9 collective-permute-start.7
  132.5 0.7 pad_add_fusion.1.table
  133.1 8.1 %all-to-all-start.3 = ((f32[16,2,256,256]{3,2,1,0:T(8,128)}), f32[16,2,256,256]{3,2,1,0:T(8,128)}, u32[]{:S(2)}, u32[]{:S(2)}) async-start(f32[16,2,256,256]{3,2,1,0:T(8,128)} %bitcast.82), calls=%async_computation.3 | async-start | bytes 16777216 | tf_op jit(solution)/shard_map/all_to_all | solution.py:54
  141.2 57.4 %factor_lead.1 = (f32[1024,1024]{1,0:T(8,128)S(1)}, bf16[1024,1024]{1,0:T(8,128)(2,1)S(1)}, bf16[1024,1024]{1,0:T(8,128)(2,1)S(1)}) custom-call(s32[1]{0:T(128)} %bitcast.29.table, f32[16,88,256]{2,1,0:T(8,128)S(1)} %all_to_all.20.own_ref, f32[16,88,256]{2,1,0:T(8,128)S(1)} %collective-permute-done.7.other_ref), custom_call_target="tpu_custom_call" | custom-call | flops 60000002048 | bytes 10485760 | tf_op jit(solution)/shard_map/factor_lead/pallas_call | solution.py:208
  198.6 1.9 copy-done.1
  200.6 1.3 copy-done.2
  201.9 1.4 copy-done.3
  203.3 84.5 %all-gather.7.cloned.1.call-done = f32[8192,256]{1,0:T(8,128)} async-done(((f32[512,256]{1,0:T(8,128)}), f32[8192,256]{1,0:T(8,128)}) %all-gather.7.cloned.1.call-update) | async-done | bytes 8388624 | tf_op jit(solution)/shard_map/all_gather | solution.py:580
  287.7 35.2 %update_front.1.base_ref = f32[2048,1024]{1,0:T(8,128)} custom-call(s32[2]{0:T(128)} %pad_add_fusion.1.table, f32[8,2,256,256]{3,2,1,0:T(8,128)} %bitcast.87, f32[8,2,256,256]{3,2,1,0:T(8,128)} %bitcast.88, f32[8,2,256,256]{3,2,1,0:T(8,128)} %bitcast.89, f32[8,2,256,256]{3,2,1,0:T(8,128)} %bitcast.90, f32[16,512,256]{2,1,0:T(8,128)} %bitcast.83, ...), custom_call_target="tpu_custom_call" | custom-call | flops 25999998976 | bytes 37748736 | tf_op jit(solution)/shard_map/update_front/pallas_call | solution.py:323
  322.9 0.5 copy.22
  323.4 0.6 fusion.notes_ref
  324.0 4.9 %add_table.1.table = s32[65]{0:T(128)} custom-call(s32[1]{0:T(128)} %bitcast.info_ref, s32[16,16]{1,0:T(8,128)} %fusion.notes_ref), custom_call_target="tpu_custom_call" | custom-call | tf_op jit(solution)/shard_map/add_table/pallas_call | solution.py:526
  329.0 0.7 copy-done
  329.6 10.4 %add_children.1 = f32[2048,1024]{1,0:T(8,128)} custom-call(s32[65]{0:T(128)S(1)} %copy-done, f32[2048,1024]{1,0:T(8,128)} %update_front.1.base_ref, f32[32,256,256]{2,1,0:T(8,128)} %bitcast.32.slot_ref), custom_call_target="tpu_custom_call", output_to_operand_aliasing={{}: (1, {})} | custom-call | flops 4000000 | bytes 25165824 | tf_op jit(solution)/shard_map/add_children/pallas_call | solution.py:543
  (34 shorter events, 0.7 us)
Async XLA Ops:
  8.2 22.9 %all-to-all-start = ((f32[16,16,256]{2,1,0:T(8,128)}), f32[16,16,256]{2,1,0:T(8,128)S(1)}, u32[]{:S(2)}, u32[]{:S(2)}) async-start(f32[16,16,256]{2,1,0:T(8,128)} %bitcast.1), calls=%async_computation | async-start | bytes 524288 | tf_op jit(solution)/shard_map/all_to_all | solution.py:54
  19.4 1.8 copy-start.4
  31.9 16.0 %all-to-all-start.1 = ((f32[8,4,16,256]{3,2,1,0:T(8,128)}), f32[8,4,16,256]{3,2,1,0:T(8,128)S(1)}, u32[]{:S(2)}, u32[]{:S(2)}) async-start(f32[8,4,16,256]{3,2,1,0:T(8,128)} %broadcast_in_dim.19), calls=%async_computation.1 | async-start | bytes 1048576 | tf_op jit(solution)/shard_map/all_to_all | solution.py:54
  38.5 164.8 %all-gather.5.cloned.1.call-start = ((), (), s32[]{:S(2)}) async-start(), calls=%async_computation.4 | async-start | bytes 4718592 | tf_op jit(solution)/shard_map/all_gather | solution.py:588
  39.5 8.6 %collective-permute-start = (f32[2,256,256]{2,1,0:T(8,128)}, f32[2,256,256]{2,1,0:T(8,128)S(1)}, u32[]{:S(2)}, u32[]{:S(2)}) collective-permute-start(f32[2,256,256]{2,1,0:T(8,128)} %pad_maximum_fusion), channel_id=1, source_target_pairs={{0,0},{1,32},{2,64},{3,96},{16,1},{17,33},{18,65},{19,97},{32,2},{... | collective-permute-start | bytes 1572872 | tf_op jit(solution)/shard_map/ppermute | solution.py:81
  41.0 7.1 %collective-permute-start.2 = (f32[2,256,256]{2,1,0:T(8,128)}, f32[2,256,256]{2,1,0:T(8,128)}, u32[]{:S(2)}, u32[]{:S(2)}) collective-permute-start(f32[2,256,256]{2,1,0:T(8,128)} %pad_maximum_fusion.2), channel_id=1, source_target_pairs={{0,8},{1,40},{2,72},{3,104},{16,9},{17,41},{18,73},{19,105},{32,10... | collective-permute-start | bytes 1572872 | tf_op jit(solution)/shard_map/ppermute | solution.py:81
  43.3 30.6 %collective-permute-start.3 = (f32[2,256,256]{2,1,0:T(8,128)}, f32[2,256,256]{2,1,0:T(8,128)}, u32[]{:S(2)}, u32[]{:S(2)}) collective-permute-start(f32[2,256,256]{2,1,0:T(8,128)} %pad_maximum_fusion.3), channel_id=1, source_target_pairs={{0,24},{1,56},{2,88},{3,120},{16,25},{17,57},{18,89},{19,121},{32,... | collective-permute-start | bytes 1572872 | tf_op jit(solution)/shard_map/ppermute | solution.py:81
  45.4 28.5 %collective-permute-start.1 = (f32[2,256,256]{2,1,0:T(8,128)}, f32[2,256,256]{2,1,0:T(8,128)}, u32[]{:S(2)}, u32[]{:S(2)}) collective-permute-start(f32[2,256,256]{2,1,0:T(8,128)} %pad_maximum_fusion.1), channel_id=1, source_target_pairs={{0,16},{1,48},{2,80},{3,112},{16,17},{17,49},{18,81},{19,113},{32,... | collective-permute-start | bytes 1572872 | tf_op jit(solution)/shard_map/ppermute | solution.py:81
  76.2 211.5 %all-gather.7.cloned.1.call-start = ((), (), s32[]{:S(2)}) async-start(), calls=%async_computation.5 | async-start | bytes 8912896 | tf_op jit(solution)/shard_map/all_gather | solution.py:580
  77.4 3.5 %collective-permute-start.4 = (f32[512,256]{1,0:T(8,128)}, f32[512,256]{1,0:T(8,128)S(1)}, u32[]{:S(2)}, u32[]{:S(2)}) collective-permute-start(f32[512,256]{1,0:T(8,128)} %get-tuple-element.39), channel_id=1, source_target_pairs={{0,4},{1,5},{2,6},{3,7},{16,20},{17,21},{18,22},{19,23},{32,36},{3... | collective-permute-start | bytes 1572872 | tf_op jit(solution)/shard_map/ppermute | solution.py:45
  78.1 13.4 %collective-permute-start.6 = (f32[512,256]{1,0:T(8,128)}, f32[512,256]{1,0:T(8,128)}, u32[]{:S(2)}, u32[]{:S(2)}) collective-permute-start(f32[512,256]{1,0:T(8,128)} %get-tuple-element.40), channel_id=1, source_target_pairs={{0,12},{1,13},{2,14},{3,15},{16,28},{17,29},{18,30},{19,31},{32,44... | collective-permute-start | bytes 1572872 | tf_op jit(solution)/shard_map/ppermute | solution.py:45
  79.4 12.1 %collective-permute-start.5 = (f32[512,256]{1,0:T(8,128)S(1)}, f32[512,256]{1,0:T(8,128)}, u32[]{:S(2)}, u32[]{:S(2)}) collective-permute-start(f32[512,256]{1,0:T(8,128)S(1)} %get-tuple-element.41), channel_id=1, source_target_pairs={{0,8},{1,9},{2,10},{3,11},{16,24},{17,25},{18,26},{19,27},{32,40},... | collective-permute-start | bytes 1572872 | tf_op jit(solution)/shard_map/ppermute | solution.py:45
  129.6 11.6 %collective-permute-start.7 = (f32[16,88,256]{2,1,0:T(8,128)S(1)}, f32[16,88,256]{2,1,0:T(8,128)S(1)}, u32[]{:S(2)}, u32[]{:S(2)}) collective-permute-start(f32[16,88,256]{2,1,0:T(8,128)S(1)} %all_to_all.20.own_ref), channel_id=1, source_target_pairs={{0,16},{16,0},{32,48},{48,32},{64,80},{80,64},{96,112},{112,96},{1... | collective-permute-start | bytes 4325384 | tf_op jit(solution)/shard_map/ppermute | solution.py:39
  133.1 195.8 %all-to-all-start.3 = ((f32[16,2,256,256]{3,2,1,0:T(8,128)}), f32[16,2,256,256]{3,2,1,0:T(8,128)}, u32[]{:S(2)}, u32[]{:S(2)}) async-start(f32[16,2,256,256]{3,2,1,0:T(8,128)} %bitcast.82), calls=%async_computation.3 | async-start | bytes 16777216 | tf_op jit(solution)/shard_map/all_to_all | solution.py:54
  198.6 1.9 copy-start.1
  200.5 1.3 copy-start.2
  201.9 1.4 copy-start.3
  329.0 0.7 copy-start
Sparse Core Ops, SparseCore 0:
  76.3 32.7 all-gather.4
  111.3 176.4 all-gather.6
where the time goes:
time: 348 us; the launch traced here: 347 us
  waiting for transfers between devices  122 us (35%)
  Pallas kernels  117 us (34%)
  blocking collectives  35.8 us (10%)
  starting transfers between devices  32.5 us (9%)
  other arithmetic  14.5 us (4%)
  between operations  13.6 us (4%)
  local copies, waits for them, and re-layouts  11.6 us (3%)
    all_gather x1, waiting for transfers between devices, on_device(): raw = lax.all_gather(after(piece, four), 'col', axis=0, tiled=False)  84.5 us
    pallas_call x1, Pallas kernels, factor_lead(): pl.pallas_call(factor_kernel, out_shape=(jax.ShapeDtypeStruct((n, n), F32...  57.4 us
    all_to_all x1, blocking collectives, exchange(): return lax.all_to_all(value, axis, split_axis=0, concat_axis=0, tiled=True)  35.8 us
    pallas_call x1, Pallas kernels, update_front(): pl.pallas_call(update_kernel, out_shape=jax.ShapeDtypeStruct((rows, cols)...  35.2 us
    ppermute x4, waiting for transfers between devices, col_pieces(): part = lax.ppermute(part, ('row', 'col'), pairs)  25.8 us
    all_to_all x3, starting transfers between devices, exchange(): return lax.all_to_all(value, axis, split_axis=0, concat_axis=0, tiled=True)  21.2 us
    ppermute x3, waiting for transfers between devices, spread_x(): lax.ppermute(parts[q], 'col', [(y, q * SIDE + y) for y in range(SIDE)])  10.6 us
    pallas_call x1, Pallas kernels, add_children(): pl.pallas_call(add_kernel, out_shape=jax.ShapeDtypeStruct(base.shape, F32...  10.4 us
  transfers between devices with their start and end apart: 13, of which 4 were waited for; matrix products, arithmetic and copies ran while one was open for 5% of the time, Pallas kernels for 31%

commit v1 on v0

--- a/solution.py
+++ b/solution.py
@@ -575,7 +575,7 @@
     late = after(slab, strip)
     rows = slab.shape[0] // SIDE
     piece = spread_x([late[q * rows : (q + 1) * rows] for q in range(SIDE)], x)
-    uc = col_pieces(late)
+    uc = col_pieces(after(late, piece))
     share, four = lead_share(strip, core)
     raw = lax.all_gather(after(piece, four), "col", axis=0, tiled=False)
     packed = map_children(child_blocks, child_target, child_place, child_live, mesh_cols)

time: 348 us -> 375 us (1.078)
  the two profiles are of different devices: /device:TPU:23 before, /device:TPU:28 now
where the time goes in v1:
time: 375 us; the launch traced here: 374 us
  waiting for transfers between devices  160 us (43%)
  Pallas kernels  117 us (31%)
  starting transfers between devices  30.8 us (8%)
  blocking collectives  30.1 us (8%)
  between operations  13.7 us (4%)
  local copies, waits for them, and re-layouts  12.3 us (3%)
  other arithmetic  10 us (3%)
    all_gather x1, waiting for transfers between devices, on_device(): raw = lax.all_gather(after(piece, four), 'col', axis=0, tiled=False)  118 us
    pallas_call x1, Pallas kernels, factor_lead(): pl.pallas_call(factor_kernel, out_shape=(jax.ShapeDtypeStruct((n, n), F32...  57.4 us
    pallas_call x1, Pallas kernels, update_front(): pl.pallas_call(update_kernel, out_shape=jax.ShapeDtypeStruct((rows, cols)...  35.2 us
    all_to_all x1, blocking collectives, exchange(): return lax.all_to_all(value, axis, split_axis=0, concat_axis=0, tiled=True)  30.1 us
    ppermute x3, waiting for transfers between devices, spread_x(): lax.ppermute(parts[q], 'col', [(y, q * SIDE + y) for y in range(SIDE)])  24.1 us
    all_to_all x3, starting transfers between devices, exchange(): return lax.all_to_all(value, axis, split_axis=0, concat_axis=0, tiled=True)  20.6 us
    ppermute x4, waiting for transfers between devices, col_pieces(): part = lax.ppermute(part, ('row', 'col'), pairs)  17.6 us
    pallas_call x1, Pallas kernels, add_children(): pl.pallas_call(add_kernel, out_shape=jax.ShapeDtypeStruct(base.shape, F32...  10.2 us
  transfers between devices with their start and end apart: 13, of which 3 were waited for; matrix products, arithmetic and copies ran while one was open for 3% of the time, Pallas kernels for 28%

profile of v1, /device:TPU:28, one launch (start us, length us, event | category | flops | bytes accessed | tf_op | source)
XLA Modules:
  0.0 373.8 jit_solution(16745438793575019691)
XLA Ops:
  6.5 1.7 slice.139
  8.2 7.1 %all-to-all-start = ((f32[16,16,256]{2,1,0:T(8,128)}), f32[16,16,256]{2,1,0:T(8,128)S(1)}, u32[]{:S(2)}, u32[]{:S(2)}) async-start(f32[16,16,256]{2,1,0:T(8,128)} %bitcast.1), calls=%async_computation | async-start | bytes 524288 | tf_op jit(solution)/shard_map/all_to_all | solution.py:54
  15.3 0.7 fusion.8
  16.0 0.7 and_select_fusion.1
  16.7 0.8 compare_reduce_fusion
  17.5 0.1 select_reduce_fusion.4
  17.7 0.2 convert_reduce_fusion.1
  17.8 0.7 multiply_add_fusion
  18.5 0.7 fusion.6
  19.2 0.8 slice_bitcast_fusion.19
  20.0 0.2 convert_reduce_fusion
  20.2 0.7 convert_element_type.23
  20.9 1.7 slice.154
  22.8 0.1 select_reduce_fusion.3
  22.9 0.7 pad_add_fusion.table
  23.6 0.9 broadcast_in_dim.19
  24.4 5.3 %all-to-all-start.1 = ((f32[8,4,16,256]{3,2,1,0:T(8,128)}), f32[8,4,16,256]{3,2,1,0:T(8,128)S(1)}, u32[]{:S(2)}, u32[]{:S(2)}) async-start(f32[8,4,16,256]{3,2,1,0:T(8,128)} %broadcast_in_dim.19), calls=%async_computation.1 | async-start | bytes 1048576 | tf_op jit(solution)/shard_map/all_to_all | solution.py:54
  29.8 8.8 %map_children.1 = f32[32,256,256]{2,1,0:T(8,128)} custom-call(s32[32]{0:T(128)} %pad_add_fusion.table, f32[8,256,256]{2,1,0:T(8,128)} %block_ref.1, s32[8,2,256]{2,1,0:T(2,128)} %place_ref.1), custom_call_target="tpu_custom_call" | custom-call | flops 2000000000 | bytes 4194304 | tf_op jit(solution)/shard_map/map_children/pallas_call | solution.py:412
  38.6 1.2 fusion.7
  39.8 0.7 collective-permute-start
  40.5 1.5 collective-permute-start.2
  42.0 1.3 collective-permute-start.1
  43.3 24.1 %collective-permute-done.1 = f32[512,256]{1,0:T(8,128)} collective-permute-done((f32[512,256]{1,0:T(8,128)}, f32[512,256]{1,0:T(8,128)}, u32[]{:S(2)}, u32[]{:S(2)}) %collective-permute-start.1) | collective-permute-done | bytes 524320 | tf_op jit(solution)/shard_map/ppermute | solution.py:45
  67.5 2.1 add_add_fusion.1
  69.6 0.1 slice_bitcast_fusion.5
  69.8 0.7 collective-permute-start.3
  70.6 1.3 collective-permute-start.5
  71.9 0.7 collective-permute-start.6
  72.6 0.7 collective-permute-start.4
  73.4 17.6 %collective-permute-done.5 = f32[2,256,256]{2,1,0:T(8,128)S(1)} collective-permute-done((f32[2,256,256]{2,1,0:T(8,128)S(1)}, f32[2,256,256]{2,1,0:T(8,128)S(1)}, u32[]{:S(2)}, u32[]{:S(2)}) %collective-permute-start.5) | collective-permute-done | bytes 524320 | tf_op jit(solution)/shard_map/ppermute | solution.py:81
  91.0 0.9 add_add_fusion
  92.0 0.7 all-gather.7.cloned.1.call-update
  92.7 0.1 broadcast_in_dim.23
  92.8 30.1 %all_to_all.20.own_ref = f32[16,88,256]{2,1,0:T(8,128)S(1)} all-to-all(f32[16,88,256]{2,1,0:T(8,128)S(1)} %broadcast_in_dim.23), channel_id=1, replica_groups=mesh['row'=8,'col'=16] {'col'}, dimensions={0} | all-to-all | bytes 2883584 | tf_op jit(solution)/shard_map/all_to_all | solution.py:54
  123.0 3.3 collective-permute-start.7
  126.3 0.6 pad_add_fusion.1.table
  126.9 8.1 %all-to-all-start.3 = ((f32[16,2,256,256]{3,2,1,0:T(8,128)}), f32[16,2,256,256]{3,2,1,0:T(8,128)}, u32[]{:S(2)}, u32[]{:S(2)}) async-start(f32[16,2,256,256]{3,2,1,0:T(8,128)} %bitcast.82), calls=%async_computation.3 | async-start | bytes 16777216 | tf_op jit(solution)/shard_map/all_to_all | solution.py:54
  135.1 57.4 %factor_lead.1 = (f32[1024,1024]{1,0:T(8,128)S(1)}, bf16[1024,1024]{1,0:T(8,128)(2,1)S(1)}, bf16[1024,1024]{1,0:T(8,128)(2,1)S(1)}) custom-call(s32[1]{0:T(128)} %bitcast.29.table, f32[16,88,256]{2,1,0:T(8,128)S(1)} %all_to_all.20.own_ref, f32[16,88,256]{2,1,0:T(8,128)S(1)} %collective-permute-done.7.other_ref), custom_call_target="tpu_custom_call" | custom-call | flops 60000002048 | bytes 10485760 | tf_op jit(solution)/shard_map/factor_lead/pallas_call | solution.py:208
  192.5 1.9 copy-done.1
  194.4 1.3 copy-done.2
  195.8 1.4 copy-done.3
  197.2 117.8 %all-gather.7.cloned.1.call-done = f32[8192,256]{1,0:T(8,128)} async-done(((f32[512,256]{1,0:T(8,128)}), f32[8192,256]{1,0:T(8,128)}) %all-gather.7.cloned.1.call-update) | async-done | bytes 8388624 | tf_op jit(solution)/shard_map/all_gather | solution.py:580
  314.9 35.2 %update_front.1.base_ref = f32[2048,1024]{1,0:T(8,128)} custom-call(s32[2]{0:T(128)} %pad_add_fusion.1.table, f32[8,2,256,256]{3,2,1,0:T(8,128)} %bitcast.87, f32[8,2,256,256]{3,2,1,0:T(8,128)} %bitcast.88, f32[8,2,256,256]{3,2,1,0:T(8,128)} %bitcast.89, f32[8,2,256,256]{3,2,1,0:T(8,128)} %bitcast.90, f32[16,512,256]{2,1,0:T(8,128)} %bitcast.83, ...), custom_call_target="tpu_custom_call" | custom-call | flops 25999998976 | bytes 37748736 | tf_op jit(solution)/shard_map/update_front/pallas_call | solution.py:323
  350.2 0.5 copy.22
  350.6 0.6 fusion.notes_ref
  351.2 5.0 %add_table.1.table = s32[65]{0:T(128)} custom-call(s32[1]{0:T(128)} %bitcast.info_ref, s32[16,16]{1,0:T(8,128)} %fusion.notes_ref), custom_call_target="tpu_custom_call" | custom-call | tf_op jit(solution)/shard_map/add_table/pallas_call | solution.py:526
  356.2 0.6 copy-done
  356.8 10.2 %add_children.1 = f32[2048,1024]{1,0:T(8,128)} custom-call(s32[65]{0:T(128)S(1)} %copy-done, f32[2048,1024]{1,0:T(8,128)} %update_front.1.base_ref, f32[32,256,256]{2,1,0:T(8,128)} %bitcast.32.slot_ref), custom_call_target="tpu_custom_call", output_to_operand_aliasing={{}: (1, {})} | custom-call | flops 4000000 | bytes 25165824 | tf_op jit(solution)/shard_map/add_children/pallas_call | solution.py:543
  (32 shorter events, 0.5 us)
Async XLA Ops:
  8.2 15.4 %all-to-all-start = ((f32[16,16,256]{2,1,0:T(8,128)}), f32[16,16,256]{2,1,0:T(8,128)S(1)}, u32[]{:S(2)}, u32[]{:S(2)}) async-start(f32[16,16,256]{2,1,0:T(8,128)} %bitcast.1), calls=%async_computation | async-start | bytes 524288 | tf_op jit(solution)/shard_map/all_to_all | solution.py:54
  24.4 18.8 %all-to-all-start.1 = ((f32[8,4,16,256]{3,2,1,0:T(8,128)}), f32[8,4,16,256]{3,2,1,0:T(8,128)S(1)}, u32[]{:S(2)}, u32[]{:S(2)}) async-start(f32[8,4,16,256]{3,2,1,0:T(8,128)} %broadcast_in_dim.19), calls=%async_computation.1 | async-start | bytes 1048576 | tf_op jit(solution)/shard_map/all_to_all | solution.py:54
  29.8 167.4 %all-gather.5.cloned.1.call-start = ((), (), s32[]{:S(2)}) async-start(), calls=%async_computation.4 | async-start | bytes 4718592 | tf_op jit(solution)/shard_map/all_gather | solution.py:588
  39.8 3.6 collective-permute-start
  40.5 2.9 collective-permute-start.2
  42.0 25.5 %collective-permute-start.1 = (f32[512,256]{1,0:T(8,128)}, f32[512,256]{1,0:T(8,128)}, u32[]{:S(2)}, u32[]{:S(2)}) collective-permute-start(f32[512,256]{1,0:T(8,128)} %get-tuple-element.51), channel_id=1, source_target_pairs={{0,8},{1,9},{2,10},{3,11},{16,24},{17,25},{18,26},{19,27},{32,40},... | collective-permute-start | bytes 1572872 | tf_op jit(solution)/shard_map/ppermute | solution.py:45
  69.8 3.6 collective-permute-start.3
  70.6 20.5 %collective-permute-start.5 = (f32[2,256,256]{2,1,0:T(8,128)S(1)}, f32[2,256,256]{2,1,0:T(8,128)S(1)}, u32[]{:S(2)}, u32[]{:S(2)}) collective-permute-start(f32[2,256,256]{2,1,0:T(8,128)S(1)} %pad_maximum_fusion.2), channel_id=1, source_target_pairs={{0,8},{1,40},{2,72},{3,104},{16,9},{17,41},{18,73},{19,105},{32,10... | collective-permute-start | bytes 1572872 | tf_op jit(solution)/shard_map/ppermute | solution.py:81
  71.9 19.1 %collective-permute-start.6 = (f32[2,256,256]{2,1,0:T(8,128)S(1)}, f32[2,256,256]{2,1,0:T(8,128)S(1)}, u32[]{:S(2)}, u32[]{:S(2)}) collective-permute-start(f32[2,256,256]{2,1,0:T(8,128)S(1)} %pad_maximum_fusion.3), channel_id=1, source_target_pairs={{0,24},{1,56},{2,88},{3,120},{16,25},{17,57},{18,89},{19,121},{32,... | collective-permute-start | bytes 1572872 | tf_op jit(solution)/shard_map/ppermute | solution.py:81
  72.6 18.4 %collective-permute-start.4 = (f32[2,256,256]{2,1,0:T(8,128)S(1)}, f32[2,256,256]{2,1,0:T(8,128)S(1)}, u32[]{:S(2)}, u32[]{:S(2)}) collective-permute-start(f32[2,256,256]{2,1,0:T(8,128)S(1)} %pad_maximum_fusion.1), channel_id=1, source_target_pairs={{0,16},{1,48},{2,80},{3,112},{16,17},{17,49},{18,81},{19,113},{32,... | collective-permute-start | bytes 1572872 | tf_op jit(solution)/shard_map/ppermute | solution.py:81
  92.0 223.0 %all-gather.7.cloned.1.call-start = ((), (), s32[]{:S(2)}) async-start(), calls=%async_computation.5 | async-start | bytes 8912896 | tf_op jit(solution)/shard_map/all_gather | solution.py:580
  123.0 12.1 %collective-permute-start.7 = (f32[16,88,256]{2,1,0:T(8,128)S(1)}, f32[16,88,256]{2,1,0:T(8,128)S(1)}, u32[]{:S(2)}, u32[]{:S(2)}) collective-permute-start(f32[16,88,256]{2,1,0:T(8,128)S(1)} %all_to_all.20.own_ref), channel_id=1, source_target_pairs={{0,16},{16,0},{32,48},{48,32},{64,80},{80,64},{96,112},{112,96},{1... | collective-permute-start | bytes 4325384 | tf_op jit(solution)/shard_map/ppermute | solution.py:39
  126.9 229.3 %all-to-all-start.3 = ((f32[16,2,256,256]{3,2,1,0:T(8,128)}), f32[16,2,256,256]{3,2,1,0:T(8,128)}, u32[]{:S(2)}, u32[]{:S(2)}) async-start(f32[16,2,256,256]{3,2,1,0:T(8,128)} %bitcast.82), calls=%async_computation.3 | async-start | bytes 16777216 | tf_op jit(solution)/shard_map/all_to_all | solution.py:54
  192.5 1.9 copy-start.1
  194.4 1.3 copy-start.2
  195.8 1.4 copy-start.3
  356.2 0.6 copy-start
Sparse Core Ops, SparseCore 0:
  92.1 44.9 all-gather.4
  139.3 175.6 all-gather.6

commit v2 on v1

--- a/solution.py
+++ b/solution.py
@@ -35,8 +35,16 @@
     return high, (value - high.astype(F32)).astype(BF16)
 
 
+def shift_z(value, dz):
+    return lax.ppermute(value, "row", [(r, (r + 2 * dz) % 8) for r in range(8)])
+
+
 def swap_cores(value):
     return lax.ppermute(value, "row", [(r, r ^ 1) for r in range(8)])
+
+
+def ring_gather(value, shift):
+    return [value, shift(value, 1), shift(value, -1), shift(value, 2)]
 
 
 def spread_x(parts, x):
@@ -68,7 +76,7 @@
     return jnp.where(core == 0, first, second), four
 
 
-def col_pieces(slab):
+def col_pieces(slab, core):
     blocks = slab.reshape(8, BLK, BLK)
     out = None
     for h in range(2):
@@ -80,7 +88,10 @@
             part = jnp.stack([blocks[4 * q + h], blocks[4 * q + 2 + h]])
             part = lax.ppermute(part, ("row", "col"), pairs)
             out = part if out is None else out + part
-    return out
+    other = swap_cores(out)
+    return jnp.concatenate(
+        [jnp.where(core == 0, out, other), jnp.where(core == 0, other, out)], axis=0
+    )
 
 
 def factor_block(a, u_ref, e_ref):
@@ -231,7 +242,11 @@
     front_ref, own_ref, high_ref, low_ref, out_ref = refs[8:13]
     ch, cl, rh, rl, pan = refs[13:]
     g = pl.program_id(0)
-    r, c = table[0], table[1]
+    r, c = table[4], table[5]
+
+    def put(rows, spot, value):
+        cols = pl.ds(pl.multiple_of(spot * BLK, BLK), BLK)
+        rh[rows, cols], rl[rows, cols] = split2(value)
 
     upper, lower = slice(0, BLK), slice(BLK, 2 * BLK)
 
@@ -252,10 +267,9 @@
 
     @pl.when(g < 2)
     def _():
-        for j in range(LEADS):
-            cols = slice(j * BLK, (j + 1) * BLK)
-            rh[upper, cols], rl[upper, cols] = split2(uc[j][0, 0])
-            rh[lower, cols], rl[lower, cols] = split2(uc[j][0, 1])
+        for q in range(SIDE):
+            put(upper, table[q], uc[q][0])
+            put(lower, table[q], uc[q][1])
         got = solve()
         at = pl.ds(pl.multiple_of(g * 2 * BLK, BLK), 2 * BLK)
         for j in range(LEADS):
@@ -309,14 +323,11 @@
     def raw_spec(j):
         return pl.BlockSpec((1, tall, BLK), lambda g, t: (step(g) * SIDE + j, 0, 0))
 
-    def uc_spec(j):
-        return pl.BlockSpec((1, 2, BLK, BLK), lambda g, t: (2 * j + jnp.minimum(g, 1), 0, 0, 0))
-
-    in_specs = [uc_spec(j) for j in range(LEADS)]
+    in_specs = [pl.BlockSpec((2, BLK, BLK), lambda g, t: (jnp.minimum(g, 1), 0, 0))] * SIDE
     in_specs += [raw_spec(j) for j in range(LEADS)]
     in_specs += [
         tall_spec(),
-        pl.BlockSpec((BLK, n), lambda g, t: (jnp.minimum(t[0], LEADS - 1), 0)),
+        pl.BlockSpec((BLK, n), lambda g, t: (jnp.minimum(t[4], LEADS - 1), 0)),
         pl.BlockSpec((n, n), lambda g, t: (0, 0)),
         pl.BlockSpec((n, n), lambda g, t: (0, 0)),
     ]
@@ -339,7 +350,7 @@
         compiler_params=pltpu.CompilerParams(vmem_limit_bytes=58 << 20),
         cost_estimate=pl.CostEstimate(flops=26_000_000_000, bytes_accessed=36 << 20, transcendentals=0),
         name="update_front",
-    )(table, *([uc] * LEADS), *([raw] * LEADS), front, factor, high, low)
+    )(table, *uc, *([raw] * LEADS), front, factor, high, low)
 
 
 def slots_of(target, mesh_cols):
@@ -351,7 +362,7 @@
     goal = target[..., 1] % mesh_cols
     alike = (goal[..., :, None] == goal[..., None, :]) & leads[..., None, :]
     rank = jnp.sum((alike & (number < first[..., :, None])).astype(I32), axis=-1)
-    return goal * CAP + rank, leads
+    return rank * mesh_cols + goal, leads
 
 
 def sort_order(keys):
@@ -426,15 +437,25 @@
     )(table, child_blocks, child_place)
 
 
-def add_kernel(table, base_ref, slot_ref, out_ref, buffers, sems, next_ref):
+def add_kernel(table, base_ref, first_ref, second_ref, out_ref, buffers, sems, next_ref):
     row = pl.program_id(0)
     total = 32
     count = table[2 * total]
     deep = buffers.shape[0]
-
-    def copy(n):
+    parts = (first_ref, second_ref)
+    each = total // len(parts)
+
+    def copy(n, part, at):
         k = lax.rem(n, deep)
-        return pltpu.make_async_copy(slot_ref.at[table[total + n]], buffers.at[k], sems.at[k])
+        return pltpu.make_async_copy(part.at[at], buffers.at[k], sems.at[k])
+
+    def start(n):
+        slot = table[total + n]
+        for q, part in enumerate(parts):
+
+            @pl.when(lax.div(slot, each) == q)
+            def _():
+                copy(n, part, slot - q * each).start()
 
     @pl.when(row == 0)
     def _():
@@ -443,7 +464,7 @@
 
             @pl.when(n < count)
             def _():
-                copy(jnp.int32(n)).start()
+                start(jnp.int32(n))
 
     out_ref[...] = base_ref[...]
 
@@ -451,13 +472,13 @@
         return (n < count) & (lax.div(table[jnp.minimum(n, total - 1)], 4) == row)
 
     def add(n):
-        copy(n).wait()
+        copy(n, first_ref, 0).wait()
         cols = pl.ds(pl.multiple_of(lax.rem(table[n], 4) * BLK, BLK), BLK)
         out_ref[:, cols] = out_ref[:, cols] + buffers[lax.rem(n, deep)]
 
         @pl.when(n + deep < count)
         def _():
-            copy(n + deep).start()
+            start(n + deep)
 
         return n + 1
 
@@ -484,8 +505,8 @@
 
             @pl.when(fresh)
             def _():
-                link[s * CAP + count] = head[tile]
-                head[tile] = s * CAP + count
+                link[count * mesh_cols + s] = head[tile]
+                head[tile] = count * mesh_cols + s
 
             return (
                 jnp.where(fresh, count + 1, count),
@@ -533,7 +554,7 @@
     )(info, notes)
 
 
-def add_children(table, base, arrived):
+def add_children(table, base, first, second):
     rows, cols = base.shape
     deep = 8
 
@@ -546,7 +567,7 @@
         grid_spec=pltpu.PrefetchScalarGridSpec(
             num_scalar_prefetch=1,
             grid=(rows // BLK,),
-            in_specs=[row_spec(), pl.BlockSpec(memory_space=pl.ANY)],
+            in_specs=[row_spec()] + [pl.BlockSpec(memory_space=pl.ANY)] * 2,
             out_specs=row_spec(),
             scratch_shapes=[
                 pltpu.VMEM((deep, BLK, BLK), F32),
@@ -558,7 +579,7 @@
         compiler_params=pltpu.CompilerParams(vmem_limit_bytes=32 << 20),
         cost_estimate=pl.CostEstimate(flops=4_000_000, bytes_accessed=24 << 20, transcendentals=0),
         name="add_children",
-    )(table, base, arrived)
+    )(table, base, first, second)
 
 
 def on_device(front_matrix, child_blocks, child_target, child_place, child_live):
@@ -566,37 +587,36 @@
     mesh_cols = lax.axis_size("col")
     row = lax.axis_index("row")
     column = lax.axis_index("col")
-    x, core = column // SIDE, row % 2
+    x, y, z, core = column // SIDE, column % SIDE, row // 2, row % 2
     slab = front_matrix[:, :BLK]
 
-    table = jnp.stack([row, column]).astype(I32)
+    offset = jnp.array([0, -1, 1, 2], I32)
+    table = jnp.concatenate([(z + offset) % SIDE, row[None], column[None]]).astype(I32)
 
     strip = exchange(slab[:BLK].reshape(mesh_cols, -1, BLK), "col")[:LEADS]
     late = after(slab, strip)
     rows = slab.shape[0] // SIDE
     piece = spread_x([late[q * rows : (q + 1) * rows] for q in range(SIDE)], x)
-    uc = col_pieces(after(late, piece))
+    uc = col_pieces(late, core)
     share, four = lead_share(strip, core)
     raw = lax.all_gather(after(piece, four), "col", axis=0, tiled=False)
     packed = map_children(child_blocks, child_target, child_place, child_live, mesh_cols)
 
     note = jnp.zeros((8, BLK), F32)
     note = note.at[0, : child_target.size].set(child_target.reshape(-1).astype(F32))
-    share, packed, uc = lax.optimization_barrier(
-        (jnp.concatenate([share, note], axis=0), packed, uc)
-    )
-    uc = lax.all_gather(uc, "row", axis=0, tiled=False)
+    share = after(jnp.concatenate([share, note], axis=0), packed)
+    uc = ring_gather(after(uc, four), shift_z)
     own = to_all(share, "col")
-    packed = after(packed, own)
-    arrived = exchange(packed.reshape(mesh_cols, CAP, BLK, BLK), "col")
-    arrived = arrived.reshape(mesh_cols * CAP, BLK, BLK)
+    first, second = packed[:mesh_cols], packed[mesh_cols:]
+    first = exchange(after(first, own), "col")
     other = swap_cores(own)
 
     factor, high, low = factor_lead(core[None].astype(I32), own, other)
+    notes = after(own, factor)[:, -8, : child_target.size].astype(I32)
+    arrivals = add_table(column[None].astype(I32), notes, mesh_rows, mesh_cols, child_target.shape[0])
+    second = exchange(after(second, factor), "col")
     base = update_front(table, uc, raw, front_matrix, factor, high, low)
-    notes = after(own, base)[:, -8, : child_target.size].astype(I32)
-    arrivals = add_table(column[None].astype(I32), notes, mesh_rows, mesh_cols, child_target.shape[0])
-    return add_children(arrivals, base, arrived)
+    return add_children(arrivals, base, first, second)
 
 
 def solution(mesh):

time: 375 us -> 333 us (0.89)
  waiting for transfers between devices: 160 us -> 79.5 us
  starting transfers between devices: 30.8 us -> 68.8 us
    all_gather x1, waiting for transfers between devices: 118 us -> 0.01 us  [on_device(): raw = lax.all_gather(after(piece, four), 'col', axis=0, tiled=False)]
    ppermute x0 -> x3, waiting for transfers between devices: none -> 35.6 us  [shift_z(): return lax.ppermute(value, 'row', [(r, (r + 2 * dz) % 8) for r in range(8)])]
    ppermute x1 -> x2, starting transfers between devices: 3.34 us -> 22.4 us  [swap_cores(): return lax.ppermute(value, 'row', [(r, r ^ 1) for r in range(8)])]
    ppermute x3, waiting for transfers between devices: 24.1 us -> 6.54 us  [spread_x(): lax.ppermute(parts[q], 'col', [(y, q * SIDE + y) for y in range(SIDE)])]
    all_to_all x3 -> x4, waiting for transfers between devices: 0.01 us -> 13.1 us  [exchange(): return lax.all_to_all(value, axis, split_axis=0, concat_axis=0, tiled=True)]
    ppermute x0 -> x3, starting transfers between devices: none -> 10.9 us  [shift_z(): return lax.ppermute(value, 'row', [(r, (r + 2 * dz) % 8) for r in range(8)])]
    all_to_all x3 -> x4, starting transfers between devices: 20.6 us -> 28.2 us  [exchange(): return lax.all_to_all(value, axis, split_axis=0, concat_axis=0, tiled=True)]
    ppermute x4, waiting for transfers between devices: 17.6 us -> 24.2 us  [col_pieces(): part = lax.ppermute(part, ('row', 'col'), pairs)]
  transfers between devices with their start and end apart: 13 -> 17, of which waited for: 3 -> 6; matrix products, arithmetic and copies ran while one was open for 3% -> 4% of each run, Pallas kernels for 28% -> 33%
where the time goes in v2:
time: 333 us; the launch traced here: 330 us
  Pallas kernels  118 us (35%)
  waiting for transfers between devices  79.5 us (24%)
  starting transfers between devices  68.8 us (21%)
  blocking collectives  28.8 us (9%)
  local copies, waits for them, and re-layouts  15 us (5%)
  between operations  13.8 us (4%)
  other arithmetic  6.36 us (2%)
    pallas_call x1, Pallas kernels, factor_lead(): pl.pallas_call(factor_kernel, out_shape=(jax.ShapeDtypeStruct((n, n), F32...  57.4 us
    pallas_call x1, Pallas kernels, update_front(): pl.pallas_call(update_kernel, out_shape=jax.ShapeDtypeStruct((rows, cols)...  36.1 us
    ppermute x3, waiting for transfers between devices, shift_z(): return lax.ppermute(value, 'row', [(r, (r + 2 * dz) % 8) for r in range(8)])  35.6 us
    all_to_all x1, blocking collectives, exchange(): return lax.all_to_all(value, axis, split_axis=0, concat_axis=0, tiled=True)  28.8 us
    all_to_all x4, starting transfers between devices, exchange(): return lax.all_to_all(value, axis, split_axis=0, concat_axis=0, tiled=True)  28.2 us
    ppermute x4, waiting for transfers between devices, col_pieces(): part = lax.ppermute(part, ('row', 'col'), pairs)  24.2 us
    ppermute x2, starting transfers between devices, swap_cores(): return lax.ppermute(value, 'row', [(r, r ^ 1) for r in range(8)])  22.4 us
    all_to_all x4, waiting for transfers between devices, exchange(): return lax.all_to_all(value, axis, split_axis=0, concat_axis=0, tiled=True)  13.1 us
  transfers between devices with their start and end apart: 17, of which 6 were waited for; matrix products, arithmetic and copies ran while one was open for 4% of the time, Pallas kernels for 33%

profile of v2, /device:TPU:28, one launch (start us, length us, event | category | flops | bytes accessed | tf_op | source)
XLA Modules:
  0.0 329.8 jit_solution(12818127934690817433)
XLA Ops:
  6.5 1.7 slice.147
  8.2 7.1 %all-to-all-start = ((f32[16,16,256]{2,1,0:T(8,128)}), f32[16,16,256]{2,1,0:T(8,128)S(1)}, u32[]{:S(2)}, u32[]{:S(2)}) async-start(f32[16,16,256]{2,1,0:T(8,128)} %bitcast.1), calls=%async_computation | async-start | bytes 524288 | tf_op jit(solution)/shard_map/all_to_all | solution.py:62
  15.3 1.7 slice.163
  17.1 2.8 all-to-all-done
  19.9 1.2 fusion.9
  21.1 0.7 collective-permute-start.9
  21.8 1.5 collective-permute-start.11
  23.3 1.3 collective-permute-start.10
  24.6 0.9 broadcast_in_dim.21
  25.4 5.3 %all-to-all-start.1 = ((f32[8,4,16,256]{3,2,1,0:T(8,128)}), f32[8,4,16,256]{3,2,1,0:T(8,128)S(1)}, u32[]{:S(2)}, u32[]{:S(2)}) async-start(f32[8,4,16,256]{3,2,1,0:T(8,128)} %broadcast_in_dim.21), calls=%async_computation.1 | async-start | bytes 1048576 | tf_op jit(solution)/shard_map/all_to_all | solution.py:62
  30.8 10.3 %all-to-all-done.1 = f32[8,4,16,256]{3,2,1,0:T(8,128)S(1)} async-done(((f32[8,4,16,256]{3,2,1,0:T(8,128)}), f32[8,4,16,256]{3,2,1,0:T(8,128)S(1)}, u32[]{:S(2)}, u32[]{:S(2)}) %all-to-all-start.1) | async-done | bytes 524320 | tf_op jit(solution)/shard_map/all_to_all | solution.py:62
  41.1 6.5 %collective-permute-done.10 = f32[512,256]{1,0:T(8,128)} collective-permute-done((f32[512,256]{1,0:T(8,128)}, f32[512,256]{1,0:T(8,128)}, u32[]{:S(2)}, u32[]{:S(2)}) %collective-permute-start.10) | collective-permute-done | bytes 524320 | tf_op jit(solution)/shard_map/ppermute | solution.py:53
  47.6 2.1 add_add_fusion
  50.0 0.1 select_reduce_fusion.4
  50.2 0.2 convert_reduce_fusion.1
  50.4 0.2 convert_reduce_fusion
  50.6 0.1 select_reduce_fusion.3
  50.8 0.7 pad_add_fusion.table
  51.4 8.8 %map_children.1 = f32[32,256,256]{2,1,0:T(8,128)} custom-call(s32[32]{0:T(128)} %pad_add_fusion.table, f32[8,256,256]{2,1,0:T(8,128)} %block_ref.1, s32[8,2,256]{2,1,0:T(2,128)} %place_ref.1), custom_call_target="tpu_custom_call" | custom-call | flops 2000000000 | bytes 4194304 | tf_op jit(solution)/shard_map/map_children/pallas_call | solution.py:423
  60.3 0.1 broadcast_in_dim.24
  60.4 28.8 %all_to_all.25.own_ref = f32[16,88,256]{2,1,0:T(8,128)S(1)} all-to-all(f32[16,88,256]{2,1,0:T(8,128)S(1)} %broadcast_in_dim.24), channel_id=1, replica_groups=mesh['row'=8,'col'=16] {'col'}, dimensions={0} | all-to-all | bytes 2883584 | tf_op jit(solution)/shard_map/all_to_all | solution.py:62
  89.2 0.1 slice_bitcast_fusion.5
  89.4 0.8 collective-permute-start.1
  90.3 1.6 collective-permute-start.3
  91.9 0.7 collective-permute-start.4
  92.6 0.7 collective-permute-start.2
  93.3 4.0 %fusion.8 = (f32[16,256,256]{2,1,0:T(8,128)}, f32[16,256,256]{2,1,0:T(8,128)}) fusion(f32[32,256,256]{2,1,0:T(8,128)S(1)} %copy-done.4), kind=kLoop, calls=%fused_computation.76 | loop fusion | bytes 16777216 | tf_op jit(solution)/shard_map/slice | solution.py:610
  97.3 24.2 %collective-permute-done.3 = f32[2,256,256]{2,1,0:T(8,128)S(1)} collective-permute-done((f32[2,256,256]{2,1,0:T(8,128)S(1)}, f32[2,256,256]{2,1,0:T(8,128)S(1)}, u32[]{:S(2)}, u32[]{:S(2)}) %collective-permute-start.3) | collective-permute-done | bytes 524320 | tf_op jit(solution)/shard_map/ppermute | solution.py:89
  121.5 0.1 add_add_fusion.1
  121.6 22.4 %collective-permute-start.5 = (f32[2,256,256]{2,1,0:T(8,128)S(1)}, f32[2,256,256]{2,1,0:T(8,128)}, u32[]{:S(2)}, u32[]{:S(2)}) collective-permute-start(f32[2,256,256]{2,1,0:T(8,128)S(1)} %add_add_fusion.1), channel_id=1, source_target_pairs={{0,16},{16,0},{32,48},{48,32},{64,80},{80,64},{96,112},{112,96},{1... | collective-permute-start | bytes 1572872 | tf_op jit(solution)/shard_map/ppermute | solution.py:43
  144.0 8.6 %all-to-all-start.3 = ((f32[16,256,256]{2,1,0:T(8,128)}), f32[16,256,256]{2,1,0:T(8,128)}, u32[]{:S(2)}, u32[]{:S(2)}) async-start(f32[16,256,256]{2,1,0:T(8,128)} %get-tuple-element.35), calls=%async_computation.3 | async-start | bytes 8388608 | tf_op jit(solution)/shard_map/all_to_all | solution.py:62
  152.5 57.4 %factor_lead.1 = (f32[1024,1024]{1,0:T(8,128)S(1)}, bf16[1024,1024]{1,0:T(8,128)(2,1)S(1)}, bf16[1024,1024]{1,0:T(8,128)(2,1)S(1)}) custom-call(s32[1]{0:T(128)} %bitcast.18.table, f32[16,88,256]{2,1,0:T(8,128)S(1)} %all_to_all.25.own_ref, f32[16,88,256]{2,1,0:T(8,128)S(1)} %collective-permute-done.other_ref), custom_call_target="tpu_custom_call" | custom-call | flops 60000002048 | bytes 10485760 | tf_op jit(solution)/shard_map/factor_lead/pallas_call | solution.py:219
  210.0 2.0 copy-done.1
  212.0 1.4 copy-done.2
  213.4 1.3 copy-done.3
  214.7 7.2 %all-to-all-start.4 = ((f32[16,256,256]{2,1,0:T(8,128)}), f32[16,256,256]{2,1,0:T(8,128)}, u32[]{:S(2)}, u32[]{:S(2)}) async-start(f32[16,256,256]{2,1,0:T(8,128)} %get-tuple-element.36), calls=%async_computation.4 | async-start | bytes 8388608 | tf_op jit(solution)/shard_map/all_to_all | solution.py:62
  222.0 1.1 broadcast_select_fusion.1
  223.1 0.1 pad_maximum_fusion.refs_0_
  223.2 8.9 %collective-permute-start.8 = (f32[4,256,256]{2,1,0:T(8,128)S(1)}, f32[4,256,256]{2,1,0:T(8,128)S(1)}, u32[]{:S(2)}, u32[]{:S(2)}) collective-permute-start(f32[4,256,256]{2,1,0:T(8,128)S(1)} %pad_maximum_fusion.refs_0_), channel_id=1, source_target_pairs={{0,64},{16,80},{32,96},{48,112},{64,0},{80,16},{96,32},{112,48},{1... | collective-permute-start | bytes 3145736 | tf_op jit(solution)/shard_map/ppermute | solution.py:39
  232.1 2.0 collective-permute-start.6
  234.2 0.7 pad_add_fusion.1.table
  234.8 0.5 copy.23
  235.3 0.6 fusion.notes_ref
  235.9 4.9 %add_table.1.table = s32[65]{0:T(128)} custom-call(s32[1]{0:T(128)} %bitcast.info_ref, s32[16,16]{1,0:T(8,128)} %fusion.notes_ref), custom_call_target="tpu_custom_call" | custom-call | tf_op jit(solution)/shard_map/add_table/pallas_call | solution.py:547
  240.8 15.4 %collective-permute-done.8.refs_3_ = f32[4,256,256]{2,1,0:T(8,128)S(1)} collective-permute-done((f32[4,256,256]{2,1,0:T(8,128)S(1)}, f32[4,256,256]{2,1,0:T(8,128)S(1)}, u32[]{:S(2)}, u32[]{:S(2)}) %collective-permute-start.8) | collective-permute-done | bytes 1048608 | tf_op jit(solution)/shard_map/ppermute | solution.py:39
  256.2 20.2 %collective-permute-done.7.refs_2_ = f32[4,256,256]{2,1,0:T(8,128)} collective-permute-done((f32[4,256,256]{2,1,0:T(8,128)S(1)}, f32[4,256,256]{2,1,0:T(8,128)}, u32[]{:S(2)}, u32[]{:S(2)}) %collective-permute-start.7) | collective-permute-done | bytes 1048608 | tf_op jit(solution)/shard_map/ppermute | solution.py:39
  276.5 36.1 %update_front.1.base_ref = f32[2048,1024]{1,0:T(8,128)} custom-call(s32[6]{0:T(128)} %pad_add_fusion.1.table, f32[4,256,256]{2,1,0:T(8,128)} %copy-done.7, f32[4,256,256]{2,1,0:T(8,128)} %collective-permute-done.6.refs_1_, f32[4,256,256]{2,1,0:T(8,128)} %collective-permute-done.7.refs_2_, f32[4,256,256]{2,1,0:T(8,128)} %copy-done.10, ...), custom_call_target="tpu_custom_call" | custom-call | flops 25999998976 | bytes 37748736 | tf_op jit(solution)/shard_map/update_front/pallas_call | solution.py:334
  312.6 10.3 %add_children.1 = f32[2048,1024]{1,0:T(8,128)} custom-call(s32[65]{0:T(128)S(1)} %copy-done, f32[2048,1024]{1,0:T(8,128)} %update_front.1.base_ref, f32[16,256,256]{2,1,0:T(8,128)} %all-to-all-done.3.first_ref, f32[16,256,256]{2,1,0:T(8,128)} %all-to-all-done.4.second_ref), custom_call_target="tpu_custom_call", output_to_operand_aliasing={{}: (1, {})} | custom-call | flops 4000000 | bytes 25165824 | tf_op jit(solution)/shard_map/add_children/pallas_call | solution.py:564
  (59 shorter events, 0.6 us)
Async XLA Ops:
  8.2 11.7 %all-to-all-start = ((f32[16,16,256]{2,1,0:T(8,128)}), f32[16,16,256]{2,1,0:T(8,128)S(1)}, u32[]{:S(2)}, u32[]{:S(2)}) async-start(f32[16,16,256]{2,1,0:T(8,128)} %bitcast.1), calls=%async_computation | async-start | bytes 524288 | tf_op jit(solution)/shard_map/all_to_all | solution.py:62
  17.0 43.2 %copy-start.5 = (f32[2048,256]{1,0:T(8,128)}, f32[2048,256]{1,0:T(8,128)S(1)}, u32[]{:S(2)}) copy-start(f32[2048,256]{1,0:T(8,128)S(1)} %slice.163) | copy-start | bytes 6291460
  17.1 32.7 %copy-start.8 = (s32[8,2]{0,1:T(2,128)S(1)}, s32[8,2]{0,1:T(2,128)}, u32[]{:S(2)}) copy-start(s32[8,2]{0,1:T(2,128)} %param.10) | copy-start | bytes 196
  17.1 33.5 %copy-start.9 = (s32[8,2]{0,1:T(2,128)S(1)}, s32[8,2]{0,1:T(2,128)}, u32[]{:S(2)}) copy-start(s32[8,2]{0,1:T(2,128)} %param.12) | copy-start | bytes 196
  21.1 20.0 %collective-permute-start.9 = (f32[512,256]{1,0:T(8,128)}, f32[512,256]{1,0:T(8,128)S(1)}, u32[]{:S(2)}, u32[]{:S(2)}) collective-permute-start(f32[512,256]{1,0:T(8,128)} %get-tuple-element.43), channel_id=1, source_target_pairs={{0,4},{1,5},{2,6},{3,7},{16,20},{17,21},{18,22},{19,23},{32,36},{3... | collective-permute-start | bytes 1572872 | tf_op jit(solution)/shard_map/ppermute | solution.py:53
  21.8 19.3 %collective-permute-start.11 = (f32[512,256]{1,0:T(8,128)}, f32[512,256]{1,0:T(8,128)}, u32[]{:S(2)}, u32[]{:S(2)}) collective-permute-start(f32[512,256]{1,0:T(8,128)} %get-tuple-element.44), channel_id=1, source_target_pairs={{0,12},{1,13},{2,14},{3,15},{16,28},{17,29},{18,30},{19,31},{32,44... | collective-permute-start | bytes 1572872 | tf_op jit(solution)/shard_map/ppermute | solution.py:53
  23.3 24.3 %collective-permute-start.10 = (f32[512,256]{1,0:T(8,128)}, f32[512,256]{1,0:T(8,128)}, u32[]{:S(2)}, u32[]{:S(2)}) collective-permute-start(f32[512,256]{1,0:T(8,128)} %get-tuple-element.45), channel_id=1, source_target_pairs={{0,8},{1,9},{2,10},{3,11},{16,24},{17,25},{18,26},{19,27},{32,40},... | collective-permute-start | bytes 1572872 | tf_op jit(solution)/shard_map/ppermute | solution.py:53
  25.4 15.7 %all-to-all-start.1 = ((f32[8,4,16,256]{3,2,1,0:T(8,128)}), f32[8,4,16,256]{3,2,1,0:T(8,128)S(1)}, u32[]{:S(2)}, u32[]{:S(2)}) async-start(f32[8,4,16,256]{3,2,1,0:T(8,128)} %broadcast_in_dim.21), calls=%async_computation.1 | async-start | bytes 1048576 | tf_op jit(solution)/shard_map/all_to_all | solution.py:62
  30.7 245.8 %all-gather.3.cloned.1.call-start = ((), (), s32[]{:S(2)}) async-start(), calls=%async_computation.5 | async-start | bytes 8912896 | tf_op jit(solution)/shard_map/all_gather | solution.py:602
  60.2 29.0 %copy-start.6 = (f32[2048,256]{1,0:T(8,128)S(1)}, f32[2048,256]{1,0:T(8,128)}, u32[]{:S(2)}) copy-start(f32[2048,256]{1,0:T(8,128)} %copy-done.5) | copy-start | bytes 6291460
  89.2 4.1 %copy-start.4 = (f32[32,256,256]{2,1,0:T(8,128)S(1)}, f32[32,256,256]{2,1,0:T(8,128)}, u32[]{:S(2)}) copy-start(f32[32,256,256]{2,1,0:T(8,128)} %map_children.1) | copy-start | bytes 25165828
  89.2 63.3 %collective-permute-start = (f32[16,88,256]{2,1,0:T(8,128)S(1)}, f32[16,88,256]{2,1,0:T(8,128)S(1)}, u32[]{:S(2)}, u32[]{:S(2)}) collective-permute-start(f32[16,88,256]{2,1,0:T(8,128)S(1)} %all_to_all.25.own_ref), channel_id=1, source_target_pairs={{0,16},{16,0},{32,48},{48,32},{64,80},{80,64},{96,112},{112,96},{1... | collective-permute-start | bytes 4325384 | tf_op jit(solution)/shard_map/ppermute | solution.py:43
  89.4 7.9 %collective-permute-start.1 = (f32[2,256,256]{2,1,0:T(8,128)S(1)}, f32[2,256,256]{2,1,0:T(8,128)S(1)}, u32[]{:S(2)}, u32[]{:S(2)}) collective-permute-start(f32[2,256,256]{2,1,0:T(8,128)S(1)} %pad_maximum_fusion.1), channel_id=1, source_target_pairs={{0,0},{1,32},{2,64},{3,96},{16,1},{17,33},{18,65},{19,97},{32,2},{... | collective-permute-start | bytes 1572872 | tf_op jit(solution)/shard_map/ppermute | solution.py:89
  90.3 31.2 %collective-permute-start.3 = (f32[2,256,256]{2,1,0:T(8,128)S(1)}, f32[2,256,256]{2,1,0:T(8,128)S(1)}, u32[]{:S(2)}, u32[]{:S(2)}) collective-permute-start(f32[2,256,256]{2,1,0:T(8,128)S(1)} %pad_maximum_fusion.3), channel_id=1, source_target_pairs={{0,8},{1,40},{2,72},{3,104},{16,9},{17,41},{18,73},{19,105},{32,10... | collective-permute-start | bytes 1572872 | tf_op jit(solution)/shard_map/ppermute | solution.py:89
  91.9 29.6 %collective-permute-start.4 = (f32[2,256,256]{2,1,0:T(8,128)S(1)}, f32[2,256,256]{2,1,0:T(8,128)S(1)}, u32[]{:S(2)}, u32[]{:S(2)}) collective-permute-start(f32[2,256,256]{2,1,0:T(8,128)S(1)} %pad_maximum_fusion.4), channel_id=1, source_target_pairs={{0,24},{1,56},{2,88},{3,120},{16,25},{17,57},{18,89},{19,121},{32,... | collective-permute-start | bytes 1572872 | tf_op jit(solution)/shard_map/ppermute | solution.py:89
  92.6 28.8 %collective-permute-start.2 = (f32[2,256,256]{2,1,0:T(8,128)S(1)}, f32[2,256,256]{2,1,0:T(8,128)S(1)}, u32[]{:S(2)}, u32[]{:S(2)}) collective-permute-start(f32[2,256,256]{2,1,0:T(8,128)S(1)} %pad_maximum_fusion.2), channel_id=1, source_target_pairs={{0,16},{1,48},{2,80},{3,112},{16,17},{17,49},{18,81},{19,113},{32,... | collective-permute-start | bytes 1572872 | tf_op jit(solution)/shard_map/ppermute | solution.py:89
  121.6 100.4 %collective-permute-start.5 = (f32[2,256,256]{2,1,0:T(8,128)S(1)}, f32[2,256,256]{2,1,0:T(8,128)}, u32[]{:S(2)}, u32[]{:S(2)}) collective-permute-start(f32[2,256,256]{2,1,0:T(8,128)S(1)} %add_add_fusion.1), channel_id=1, source_target_pairs={{0,16},{16,0},{32,48},{48,32},{64,80},{80,64},{96,112},{112,96},{1... | collective-permute-start | bytes 1572872 | tf_op jit(solution)/shard_map/ppermute | solution.py:43
  144.0 70.8 %all-to-all-start.3 = ((f32[16,256,256]{2,1,0:T(8,128)}), f32[16,256,256]{2,1,0:T(8,128)}, u32[]{:S(2)}, u32[]{:S(2)}) async-start(f32[16,256,256]{2,1,0:T(8,128)} %get-tuple-element.35), calls=%async_computation.3 | async-start | bytes 8388608 | tf_op jit(solution)/shard_map/all_to_all | solution.py:62
  210.0 2.0 copy-start.1
  212.0 1.4 copy-start.2
  213.4 1.3 copy-start.3
  214.7 97.9 %all-to-all-start.4 = ((f32[16,256,256]{2,1,0:T(8,128)}), f32[16,256,256]{2,1,0:T(8,128)}, u32[]{:S(2)}, u32[]{:S(2)}) async-start(f32[16,256,256]{2,1,0:T(8,128)} %get-tuple-element.36), calls=%async_computation.4 | async-start | bytes 8388608 | tf_op jit(solution)/shard_map/all_to_all | solution.py:62
  221.9 12.2 %copy-start.11 = (s32[4]{0:T(128)S(1)}, s32[4]{0:T(128)}, u32[]{:S(2)}) copy-start(s32[4]{0:T(128)} %constant.113.clone) | copy-start | bytes 52
  223.2 53.3 %copy-start.7 = (f32[4,256,256]{2,1,0:T(8,128)}, f32[4,256,256]{2,1,0:T(8,128)S(1)}, u32[]{:S(2)}) copy-start(f32[4,256,256]{2,1,0:T(8,128)S(1)} %pad_maximum_fusion.refs_0_) | copy-start | bytes 3145732
  223.2 33.0 %collective-permute-start.8 = (f32[4,256,256]{2,1,0:T(8,128)S(1)}, f32[4,256,256]{2,1,0:T(8,128)S(1)}, u32[]{:S(2)}, u32[]{:S(2)}) collective-permute-start(f32[4,256,256]{2,1,0:T(8,128)S(1)} %pad_maximum_fusion.refs_0_), channel_id=1, source_target_pairs={{0,64},{16,80},{32,96},{48,112},{64,0},{80,16},{96,32},{112,48},{1... | collective-permute-start | bytes 3145736 | tf_op jit(solution)/shard_map/ppermute | solution.py:39
  232.1 44.3 %collective-permute-start.7 = (f32[4,256,256]{2,1,0:T(8,128)S(1)}, f32[4,256,256]{2,1,0:T(8,128)}, u32[]{:S(2)}, u32[]{:S(2)}) collective-permute-start(f32[4,256,256]{2,1,0:T(8,128)S(1)} %pad_maximum_fusion.refs_0_), channel_id=1, source_target_pairs={{0,96},{16,112},{32,0},{48,16},{64,32},{80,48},{96,64},{112,80},{1... | collective-permute-start | bytes 3145736 | tf_op jit(solution)/shard_map/ppermute | solution.py:39
  232.1 44.3 %collective-permute-start.6 = (f32[4,256,256]{2,1,0:T(8,128)S(1)}, f32[4,256,256]{2,1,0:T(8,128)}, u32[]{:S(2)}, u32[]{:S(2)}) collective-permute-start(f32[4,256,256]{2,1,0:T(8,128)S(1)} %pad_maximum_fusion.refs_0_), channel_id=1, source_target_pairs={{0,32},{16,48},{32,64},{48,80},{64,96},{80,112},{96,0},{112,16},{1... | collective-permute-start | bytes 3145736 | tf_op jit(solution)/shard_map/ppermute | solution.py:39
  256.2 20.2 %copy-start.10 = (f32[4,256,256]{2,1,0:T(8,128)}, f32[4,256,256]{2,1,0:T(8,128)S(1)}, u32[]{:S(2)}) copy-start(f32[4,256,256]{2,1,0:T(8,128)S(1)} %collective-permute-done.8.refs_3_) | copy-start | bytes 3145732
  276.5 36.1 %copy-start = (s32[65]{0:T(128)S(1)}, s32[65]{0:T(128)}, u32[]{:S(2)}) copy-start(s32[65]{0:T(128)} %add_table.1.table) | copy-start | bytes 784
Sparse Core Ops, SparseCore 0:
  49.9 128.7 all-gather.2

commit v3 on v2

--- a/solution.py
+++ b/solution.py
@@ -605,16 +605,19 @@
     note = jnp.zeros((8, BLK), F32)
     note = note.at[0, : child_target.size].set(child_target.reshape(-1).astype(F32))
     share = after(jnp.concatenate([share, note], axis=0), packed)
-    uc = ring_gather(after(uc, four), shift_z)
+    uc = after(uc, four)
     own = to_all(share, "col")
     first, second = packed[:mesh_cols], packed[mesh_cols:]
-    first = exchange(after(first, own), "col")
+    first, uc = lax.optimization_barrier((first, uc, own))[:2]
+    uc = ring_gather(uc, shift_z)
+    first = exchange(first, "col")
     other = swap_cores(own)
 
     factor, high, low = factor_lead(core[None].astype(I32), own, other)
     notes = after(own, factor)[:, -8, : child_target.size].astype(I32)
     arrivals = add_table(column[None].astype(I32), notes, mesh_rows, mesh_cols, child_target.shape[0])
-    second = exchange(after(second, factor), "col")
+    second, *uc = lax.optimization_barrier((second, *uc, factor))[:-1]
+    second = exchange(second, "col")
     base = update_front(table, uc, raw, front_matrix, factor, high, low)
     return add_children(arrivals, base, first, second)
 

time: 333 us -> 303 us (0.910)
  blocking collectives: 28.8 us -> 0 us
  starting transfers between devices: 68.8 us -> 59.3 us
  local copies, waits for them, and re-layouts: 15 us -> 19.9 us
  other arithmetic: 6.36 us -> 11 us
    all_to_all x4 -> x5, waiting for transfers between devices: 13.1 us -> 60.4 us  [exchange(): return lax.all_to_all(value, axis, split_axis=0, concat_axis=0, tiled=True)]
    ppermute x3, waiting for transfers between devices: 35.6 us -> 0.01 us  [shift_z(): return lax.ppermute(value, 'row', [(r, (r + 2 * dz) % 8) for r in range(8)])]
    all_to_all x1 -> x0, blocking collectives: 28.8 us -> none  [exchange(): return lax.all_to_all(value, axis, split_axis=0, concat_axis=0, tiled=True)]
    ppermute x4, waiting for transfers between devices: 24.2 us -> 11.8 us  [col_pieces(): part = lax.ppermute(part, ('row', 'col'), pairs)]
    ppermute x2, starting transfers between devices: 22.4 us -> 11.1 us  [swap_cores(): return lax.ppermute(value, 'row', [(r, r ^ 1) for r in range(8)])]
    all_to_all x4 -> x5, starting transfers between devices: 28.2 us -> 35.3 us  [exchange(): return lax.all_to_all(value, axis, split_axis=0, concat_axis=0, tiled=True)]
    ppermute x3, starting transfers between devices: 10.9 us -> 4.54 us  [shift_z(): return lax.ppermute(value, 'row', [(r, (r + 2 * dz) % 8) for r in range(8)])]
    slice x1, local copies, waits for them, and re-layouts: 3.95 us -> 7.71 us  [on_device(): first, second = (packed[:mesh_cols], packed[mesh_cols:])]
  transfers between devices with their start and end apart: 17 -> 18, of which waited for: 6 -> 7; matrix products, arithmetic and copies ran while one was open for 4% -> 7% of each run, Pallas kernels for 33% -> 36%
where the time goes in v3:
time: 303 us; the launch traced here: 299 us
  Pallas kernels  117 us (39%)
  waiting for transfers between devices  78.8 us (26%)
  starting transfers between devices  59.3 us (20%)
  local copies, waits for them, and re-layouts  19.9 us (7%)
  between operations  13.7 us (5%)
  other arithmetic  11 us (4%)
    all_to_all x5, waiting for transfers between devices, exchange(): return lax.all_to_all(value, axis, split_axis=0, concat_axis=0, tiled=True)  60.4 us
    pallas_call x1, Pallas kernels, factor_lead(): pl.pallas_call(factor_kernel, out_shape=(jax.ShapeDtypeStruct((n, n), F32...  57.4 us
    pallas_call x1, Pallas kernels, update_front(): pl.pallas_call(update_kernel, out_shape=jax.ShapeDtypeStruct((rows, cols)...  36.1 us
    all_to_all x5, starting transfers between devices, exchange(): return lax.all_to_all(value, axis, split_axis=0, concat_axis=0, tiled=True)  35.3 us
    ppermute x4, waiting for transfers between devices, col_pieces(): part = lax.ppermute(part, ('row', 'col'), pairs)  11.8 us
    ppermute x2, starting transfers between devices, swap_cores(): return lax.ppermute(value, 'row', [(r, r ^ 1) for r in range(8)])  11.1 us
    pallas_call x1, Pallas kernels, add_children(): pl.pallas_call(add_kernel, out_shape=jax.ShapeDtypeStruct(base.shape, F32...  9.26 us
    pallas_call x1, Pallas kernels, map_children(): pl.pallas_call(map_kernel, out_shape=jax.ShapeDtypeStruct((mesh_cols * CA...  8.77 us
  transfers between devices with their start and end apart: 18, of which 7 were waited for; matrix products, arithmetic and copies ran while one was open for 7% of the time, Pallas kernels for 36%

profile of v3, /device:TPU:28, one launch (start us, length us, event | category | flops | bytes accessed | tf_op | source)
XLA Modules:
  0.0 299.3 jit_solution(13623896058973414180)
XLA Ops:
  6.5 1.7 slice.147
  8.2 7.1 %all-to-all-start = ((f32[16,16,256]{2,1,0:T(8,128)}), f32[16,16,256]{2,1,0:T(8,128)S(1)}, u32[]{:S(2)}, u32[]{:S(2)}) async-start(f32[16,16,256]{2,1,0:T(8,128)} %bitcast.1), calls=%async_computation | async-start | bytes 524288 | tf_op jit(solution)/shard_map/all_to_all | solution.py:62
  15.3 1.7 slice.165
  17.1 2.9 all-to-all-done
  19.9 1.2 fusion.9
  21.1 0.7 collective-permute-start.9
  21.8 1.5 collective-permute-start.11
  23.3 1.3 collective-permute-start.10
  24.6 0.9 broadcast_in_dim.21
  25.4 5.3 %all-to-all-start.1 = ((f32[8,4,16,256]{3,2,1,0:T(8,128)}), f32[8,4,16,256]{3,2,1,0:T(8,128)S(1)}, u32[]{:S(2)}, u32[]{:S(2)}) async-start(f32[8,4,16,256]{3,2,1,0:T(8,128)} %broadcast_in_dim.21), calls=%async_computation.1 | async-start | bytes 1048576 | tf_op jit(solution)/shard_map/all_to_all | solution.py:62
  30.8 10.3 %all-to-all-done.1 = f32[8,4,16,256]{3,2,1,0:T(8,128)S(1)} async-done(((f32[8,4,16,256]{3,2,1,0:T(8,128)}), f32[8,4,16,256]{3,2,1,0:T(8,128)S(1)}, u32[]{:S(2)}, u32[]{:S(2)}) %all-to-all-start.1) | async-done | bytes 524320 | tf_op jit(solution)/shard_map/all_to_all | solution.py:62
  41.1 6.5 %collective-permute-done.10 = f32[512,256]{1,0:T(8,128)} collective-permute-done((f32[512,256]{1,0:T(8,128)}, f32[512,256]{1,0:T(8,128)}, u32[]{:S(2)}, u32[]{:S(2)}) %collective-permute-start.10) | collective-permute-done | bytes 524320 | tf_op jit(solution)/shard_map/ppermute | solution.py:53
  47.6 2.1 add_add_fusion
  50.2 0.2 convert_reduce_fusion.1
  50.8 0.7 pad_add_fusion.table
  51.4 8.8 %map_children.1 = f32[32,256,256]{2,1,0:T(8,128)} custom-call(s32[32]{0:T(128)} %pad_add_fusion.table, f32[8,256,256]{2,1,0:T(8,128)} %block_ref.1, s32[8,2,256]{2,1,0:T(2,128)} %place_ref.1), custom_call_target="tpu_custom_call" | custom-call | flops 2000000000 | bytes 4194304 | tf_op jit(solution)/shard_map/map_children/pallas_call | solution.py:423
  60.3 1.3 broadcast_in_dim.24
  61.5 7.5 %all-to-all-start.2 = ((f32[16,88,256]{2,1,0:T(8,128)}), f32[16,88,256]{2,1,0:T(8,128)S(1)}, u32[]{:S(2)}, u32[]{:S(2)}) async-start(f32[16,88,256]{2,1,0:T(8,128)} %broadcast_in_dim.24), calls=%async_computation.2 | async-start | bytes 2883584 | tf_op jit(solution)/shard_map/all_to_all | solution.py:62
  69.2 0.9 pad_maximum_fusion.1
  70.1 0.7 collective-permute-start.1
  70.8 0.8 pad_maximum_fusion.3
  71.6 1.3 collective-permute-start.3
  72.9 0.8 pad_maximum_fusion.4
  73.7 1.5 collective-permute-start.4
  75.2 0.9 pad_maximum_fusion.2
  76.0 1.5 collective-permute-start.2
  77.5 13.2 %all-to-all-done.2.own_ref = f32[16,88,256]{2,1,0:T(8,128)S(1)} async-done(((f32[16,88,256]{2,1,0:T(8,128)}), f32[16,88,256]{2,1,0:T(8,128)S(1)}, u32[]{:S(2)}, u32[]{:S(2)}) %all-to-all-start.2) | async-done | bytes 1441824 | tf_op jit(solution)/shard_map/all_to_all | solution.py:62
  90.7 11.8 %collective-permute-done.3 = f32[2,256,256]{2,1,0:T(8,128)} collective-permute-done((f32[2,256,256]{2,1,0:T(8,128)}, f32[2,256,256]{2,1,0:T(8,128)}, u32[]{:S(2)}, u32[]{:S(2)}) %collective-permute-start.3) | collective-permute-done | bytes 524320 | tf_op jit(solution)/shard_map/ppermute | solution.py:89
  102.5 1.7 add_add_fusion.1
  104.2 11.1 %collective-permute-start.5 = (f32[2,256,256]{2,1,0:T(8,128)S(1)}, f32[2,256,256]{2,1,0:T(8,128)S(1)}, u32[]{:S(2)}, u32[]{:S(2)}) collective-permute-start(f32[2,256,256]{2,1,0:T(8,128)S(1)} %add_add_fusion.1), channel_id=1, source_target_pairs={{0,16},{16,0},{32,48},{48,32},{64,80},{80,64},{96,112},{112,96},{1... | collective-permute-start | bytes 1572872 | tf_op jit(solution)/shard_map/ppermute | solution.py:43
  115.3 7.7 %fusion.8 = (f32[16,256,256]{2,1,0:T(8,128)}, f32[16,256,256]{2,1,0:T(8,128)}) fusion(f32[32,256,256]{2,1,0:T(8,128)} %map_children.1), kind=kLoop, calls=%fused_computation.76 | loop fusion | bytes 16777216 | tf_op jit(solution)/shard_map/slice | solution.py:610
  123.1 1.1 pad_maximum_fusion.refs_0_
  124.2 0.2 collective-permute-start.8
  124.4 4.3 %collective-permute-start.7 = (f32[4,256,256]{2,1,0:T(8,128)}, f32[4,256,256]{2,1,0:T(8,128)}, u32[]{:S(2)}, u32[]{:S(2)}) collective-permute-start(f32[4,256,256]{2,1,0:T(8,128)} %pad_maximum_fusion.refs_0_), channel_id=1, source_target_pairs={{0,96},{16,112},{32,0},{48,16},{64,32},{80,48},{96,64},{112,80},{1... | collective-permute-start | bytes 3145736 | tf_op jit(solution)/shard_map/ppermute | solution.py:39
  128.7 8.2 %all-to-all-start.3 = ((f32[16,256,256]{2,1,0:T(8,128)}), f32[16,256,256]{2,1,0:T(8,128)}, u32[]{:S(2)}, u32[]{:S(2)}) async-start(f32[16,256,256]{2,1,0:T(8,128)} %get-tuple-element.45), calls=%async_computation.3 | async-start | bytes 8388608 | tf_op jit(solution)/shard_map/all_to_all | solution.py:62
  136.9 57.4 %factor_lead.1 = (f32[1024,1024]{1,0:T(8,128)S(1)}, bf16[1024,1024]{1,0:T(8,128)(2,1)S(1)}, bf16[1024,1024]{1,0:T(8,128)(2,1)S(1)}) custom-call(s32[1]{0:T(128)} %bitcast.18.table, f32[16,88,256]{2,1,0:T(8,128)S(1)} %all-to-all-done.2.own_ref, f32[16,88,256]{2,1,0:T(8,128)S(1)} %collective-permute-done.other_ref), custom_call_target="tpu_custom_call" | custom-call | flops 60000002048 | bytes 10485760 | tf_op jit(solution)/shard_map/factor_lead/pallas_call | solution.py:219
  194.4 2.0 copy-done.1
  196.3 1.4 copy-done.2
  197.7 1.3 copy-done.3
  199.1 15.7 %all-to-all-done.3.first_ref = f32[16,256,256]{2,1,0:T(8,128)} async-done(((f32[16,256,256]{2,1,0:T(8,128)}), f32[16,256,256]{2,1,0:T(8,128)}, u32[]{:S(2)}, u32[]{:S(2)}) %all-to-all-start.3) | async-done | bytes 4194336 | tf_op jit(solution)/shard_map/all_to_all | solution.py:62
  214.8 7.2 %all-to-all-start.4 = ((f32[16,256,256]{2,1,0:T(8,128)}), f32[16,256,256]{2,1,0:T(8,128)}, u32[]{:S(2)}, u32[]{:S(2)}) async-start(f32[16,256,256]{2,1,0:T(8,128)} %get-tuple-element.46), calls=%async_computation.4 | async-start | bytes 8388608 | tf_op jit(solution)/shard_map/all_to_all | solution.py:62
  222.0 0.7 pad_add_fusion.1.table
  222.7 0.5 copy.23
  223.2 0.6 fusion.notes_ref
  223.8 5.0 %add_table.1.table = s32[65]{0:T(128)} custom-call(s32[1]{0:T(128)} %bitcast.info_ref, s32[16,16]{1,0:T(8,128)} %fusion.notes_ref), custom_call_target="tpu_custom_call" | custom-call | tf_op jit(solution)/shard_map/add_table/pallas_call | solution.py:547
  228.8 36.1 %update_front.1.base_ref = f32[2048,1024]{1,0:T(8,128)} custom-call(s32[6]{0:T(128)} %pad_add_fusion.1.table, f32[4,256,256]{2,1,0:T(8,128)} %pad_maximum_fusion.refs_0_, f32[4,256,256]{2,1,0:T(8,128)} %collective-permute-done.6.refs_1_, f32[4,256,256]{2,1,0:T(8,128)} %collective-permute-done.7.refs_2_, f32[4,256,256]{2,1,0:T(8,128)} %collective-permute-done.8.refs_3_, ...), custom_call_target="tpu_custom_call" | custom-call | flops 25999998976 | bytes 37748736 | tf_op jit(solution)/shard_map/update_front/pallas_call | solution.py:334
  264.9 18.3 %all-to-all-done.4.second_ref = f32[16,256,256]{2,1,0:T(8,128)} async-done(((f32[16,256,256]{2,1,0:T(8,128)}), f32[16,256,256]{2,1,0:T(8,128)}, u32[]{:S(2)}, u32[]{:S(2)}) %all-to-all-start.4) | async-done | bytes 4194336 | tf_op jit(solution)/shard_map/all_to_all | solution.py:62
  283.2 9.3 %add_children.1 = f32[2048,1024]{1,0:T(8,128)} custom-call(s32[65]{0:T(128)S(1)} %copy-done, f32[2048,1024]{1,0:T(8,128)} %update_front.1.base_ref, f32[16,256,256]{2,1,0:T(8,128)} %all-to-all-done.3.first_ref, f32[16,256,256]{2,1,0:T(8,128)} %all-to-all-done.4.second_ref), custom_call_target="tpu_custom_call", output_to_operand_aliasing={{}: (1, {})} | custom-call | flops 4000000 | bytes 25165824 | tf_op jit(solution)/shard_map/add_children/pallas_call | solution.py:564
  (52 shorter events, 1.2 us)
Async XLA Ops:
  8.2 11.7 %all-to-all-start = ((f32[16,16,256]{2,1,0:T(8,128)}), f32[16,16,256]{2,1,0:T(8,128)S(1)}, u32[]{:S(2)}, u32[]{:S(2)}) async-start(f32[16,16,256]{2,1,0:T(8,128)} %bitcast.1), calls=%async_computation | async-start | bytes 524288 | tf_op jit(solution)/shard_map/all_to_all | solution.py:62
  17.0 32.7 %copy-start.5 = (s32[8,2]{0,1:T(2,128)S(1)}, s32[8,2]{0,1:T(2,128)}, u32[]{:S(2)}) copy-start(s32[8,2]{0,1:T(2,128)} %param.10) | copy-start | bytes 196
  17.1 33.5 %copy-start.6 = (s32[8,2]{0,1:T(2,128)S(1)}, s32[8,2]{0,1:T(2,128)}, u32[]{:S(2)}) copy-start(s32[8,2]{0,1:T(2,128)} %param.12) | copy-start | bytes 196
  21.1 20.0 %collective-permute-start.9 = (f32[512,256]{1,0:T(8,128)}, f32[512,256]{1,0:T(8,128)S(1)}, u32[]{:S(2)}, u32[]{:S(2)}) collective-permute-start(f32[512,256]{1,0:T(8,128)} %get-tuple-element.53), channel_id=1, source_target_pairs={{0,4},{1,5},{2,6},{3,7},{16,20},{17,21},{18,22},{19,23},{32,36},{3... | collective-permute-start | bytes 1572872 | tf_op jit(solution)/shard_map/ppermute | solution.py:53
  21.8 19.3 %collective-permute-start.11 = (f32[512,256]{1,0:T(8,128)}, f32[512,256]{1,0:T(8,128)}, u32[]{:S(2)}, u32[]{:S(2)}) collective-permute-start(f32[512,256]{1,0:T(8,128)} %get-tuple-element.54), channel_id=1, source_target_pairs={{0,12},{1,13},{2,14},{3,15},{16,28},{17,29},{18,30},{19,31},{32,44... | collective-permute-start | bytes 1572872 | tf_op jit(solution)/shard_map/ppermute | solution.py:53
  23.3 24.3 %collective-permute-start.10 = (f32[512,256]{1,0:T(8,128)}, f32[512,256]{1,0:T(8,128)}, u32[]{:S(2)}, u32[]{:S(2)}) collective-permute-start(f32[512,256]{1,0:T(8,128)} %get-tuple-element.55), channel_id=1, source_target_pairs={{0,8},{1,9},{2,10},{3,11},{16,24},{17,25},{18,26},{19,27},{32,40},... | collective-permute-start | bytes 1572872 | tf_op jit(solution)/shard_map/ppermute | solution.py:53
  25.4 15.7 %all-to-all-start.1 = ((f32[8,4,16,256]{3,2,1,0:T(8,128)}), f32[8,4,16,256]{3,2,1,0:T(8,128)S(1)}, u32[]{:S(2)}, u32[]{:S(2)}) async-start(f32[8,4,16,256]{3,2,1,0:T(8,128)} %broadcast_in_dim.21), calls=%async_computation.1 | async-start | bytes 1048576 | tf_op jit(solution)/shard_map/all_to_all | solution.py:62
  30.7 198.0 %all-gather.3.cloned.1.call-start = ((), (), s32[]{:S(2)}) async-start(), calls=%async_computation.5 | async-start | bytes 8912896 | tf_op jit(solution)/shard_map/all_gather | solution.py:602
  61.5 29.1 %all-to-all-start.2 = ((f32[16,88,256]{2,1,0:T(8,128)}), f32[16,88,256]{2,1,0:T(8,128)S(1)}, u32[]{:S(2)}, u32[]{:S(2)}) async-start(f32[16,88,256]{2,1,0:T(8,128)} %broadcast_in_dim.24), calls=%async_computation.2 | async-start | bytes 2883584 | tf_op jit(solution)/shard_map/all_to_all | solution.py:62
  70.1 20.6 %collective-permute-start.1 = (f32[2,256,256]{2,1,0:T(8,128)}, f32[2,256,256]{2,1,0:T(8,128)S(1)}, u32[]{:S(2)}, u32[]{:S(2)}) collective-permute-start(f32[2,256,256]{2,1,0:T(8,128)} %pad_maximum_fusion.1), channel_id=1, source_target_pairs={{0,0},{1,32},{2,64},{3,96},{16,1},{17,33},{18,65},{19,97},{32,2},{... | collective-permute-start | bytes 1572872 | tf_op jit(solution)/shard_map/ppermute | solution.py:89
  71.6 30.9 %collective-permute-start.3 = (f32[2,256,256]{2,1,0:T(8,128)}, f32[2,256,256]{2,1,0:T(8,128)}, u32[]{:S(2)}, u32[]{:S(2)}) collective-permute-start(f32[2,256,256]{2,1,0:T(8,128)} %pad_maximum_fusion.3), channel_id=1, source_target_pairs={{0,8},{1,40},{2,72},{3,104},{16,9},{17,41},{18,73},{19,105},{32,10... | collective-permute-start | bytes 1572872 | tf_op jit(solution)/shard_map/ppermute | solution.py:89
  73.7 28.8 %collective-permute-start.4 = (f32[2,256,256]{2,1,0:T(8,128)}, f32[2,256,256]{2,1,0:T(8,128)}, u32[]{:S(2)}, u32[]{:S(2)}) collective-permute-start(f32[2,256,256]{2,1,0:T(8,128)} %pad_maximum_fusion.4), channel_id=1, source_target_pairs={{0,24},{1,56},{2,88},{3,120},{16,25},{17,57},{18,89},{19,121},{32,... | collective-permute-start | bytes 1572872 | tf_op jit(solution)/shard_map/ppermute | solution.py:89
  76.0 26.5 %collective-permute-start.2 = (f32[2,256,256]{2,1,0:T(8,128)}, f32[2,256,256]{2,1,0:T(8,128)}, u32[]{:S(2)}, u32[]{:S(2)}) collective-permute-start(f32[2,256,256]{2,1,0:T(8,128)} %pad_maximum_fusion.2), channel_id=1, source_target_pairs={{0,16},{1,48},{2,80},{3,112},{16,17},{17,49},{18,81},{19,113},{32,... | collective-permute-start | bytes 1572872 | tf_op jit(solution)/shard_map/ppermute | solution.py:89
  90.7 46.2 %collective-permute-start = (f32[16,88,256]{2,1,0:T(8,128)S(1)}, f32[16,88,256]{2,1,0:T(8,128)S(1)}, u32[]{:S(2)}, u32[]{:S(2)}) collective-permute-start(f32[16,88,256]{2,1,0:T(8,128)S(1)} %all-to-all-done.2.own_ref), channel_id=1, source_target_pairs={{0,16},{16,0},{32,48},{48,32},{64,80},{80,64},{96,112},{112,96},{1... | collective-permute-start | bytes 4325384 | tf_op jit(solution)/shard_map/ppermute | solution.py:43
  90.7 11.8 %copy-start.4 = (f32[2,256,256]{2,1,0:T(8,128)}, f32[2,256,256]{2,1,0:T(8,128)S(1)}, u32[]{:S(2)}) copy-start(f32[2,256,256]{2,1,0:T(8,128)S(1)} %collective-permute-done.1) | copy-start | bytes 1572868
  104.2 18.8 %collective-permute-start.5 = (f32[2,256,256]{2,1,0:T(8,128)S(1)}, f32[2,256,256]{2,1,0:T(8,128)S(1)}, u32[]{:S(2)}, u32[]{:S(2)}) collective-permute-start(f32[2,256,256]{2,1,0:T(8,128)S(1)} %add_add_fusion.1), channel_id=1, source_target_pairs={{0,16},{16,0},{32,48},{48,32},{64,80},{80,64},{96,112},{112,96},{1... | collective-permute-start | bytes 1572872 | tf_op jit(solution)/shard_map/ppermute | solution.py:43
  124.2 74.9 %collective-permute-start.8 = (f32[4,256,256]{2,1,0:T(8,128)}, f32[4,256,256]{2,1,0:T(8,128)}, u32[]{:S(2)}, u32[]{:S(2)}) collective-permute-start(f32[4,256,256]{2,1,0:T(8,128)} %pad_maximum_fusion.refs_0_), channel_id=1, source_target_pairs={{0,64},{16,80},{32,96},{48,112},{64,0},{80,16},{96,32},{112,48},{1... | collective-permute-start | bytes 3145736 | tf_op jit(solution)/shard_map/ppermute | solution.py:39
  124.4 74.7 %collective-permute-start.7 = (f32[4,256,256]{2,1,0:T(8,128)}, f32[4,256,256]{2,1,0:T(8,128)}, u32[]{:S(2)}, u32[]{:S(2)}) collective-permute-start(f32[4,256,256]{2,1,0:T(8,128)} %pad_maximum_fusion.refs_0_), channel_id=1, source_target_pairs={{0,96},{16,112},{32,0},{48,16},{64,32},{80,48},{96,64},{112,80},{1... | collective-permute-start | bytes 3145736 | tf_op jit(solution)/shard_map/ppermute | solution.py:39
  128.7 70.4 %collective-permute-start.6 = (f32[4,256,256]{2,1,0:T(8,128)}, f32[4,256,256]{2,1,0:T(8,128)}, u32[]{:S(2)}, u32[]{:S(2)}) collective-permute-start(f32[4,256,256]{2,1,0:T(8,128)} %pad_maximum_fusion.refs_0_), channel_id=1, source_target_pairs={{0,32},{16,48},{32,64},{48,80},{64,96},{80,112},{96,0},{112,16},{1... | collective-permute-start | bytes 3145736 | tf_op jit(solution)/shard_map/ppermute | solution.py:39
  128.7 86.1 %all-to-all-start.3 = ((f32[16,256,256]{2,1,0:T(8,128)}), f32[16,256,256]{2,1,0:T(8,128)}, u32[]{:S(2)}, u32[]{:S(2)}) async-start(f32[16,256,256]{2,1,0:T(8,128)} %get-tuple-element.45), calls=%async_computation.3 | async-start | bytes 8388608 | tf_op jit(solution)/shard_map/all_to_all | solution.py:62
  194.3 2.0 copy-start.1
  196.3 1.4 copy-start.2
  197.7 1.3 copy-start.3
  199.1 22.9 %copy-start.7 = (s32[4]{0:T(128)S(1)}, s32[4]{0:T(128)}, u32[]{:S(2)}) copy-start(s32[4]{0:T(128)} %constant.113.clone) | copy-start | bytes 52
  214.8 68.4 %all-to-all-start.4 = ((f32[16,256,256]{2,1,0:T(8,128)}), f32[16,256,256]{2,1,0:T(8,128)}, u32[]{:S(2)}, u32[]{:S(2)}) async-start(f32[16,256,256]{2,1,0:T(8,128)} %get-tuple-element.46), calls=%async_computation.4 | async-start | bytes 8388608 | tf_op jit(solution)/shard_map/all_to_all | solution.py:62
  228.7 54.4 %copy-start = (s32[65]{0:T(128)S(1)}, s32[65]{0:T(128)}, u32[]{:S(2)}) copy-start(s32[65]{0:T(128)} %add_table.1.table) | copy-start | bytes 784
Sparse Core Ops, SparseCore 0:
  49.9 144.7 all-gather.2

commit v4 on v3

--- a/solution.py
+++ b/solution.py
@@ -376,7 +376,7 @@
     return lambda values: jnp.sum(hot * values[None, :], axis=1)
 
 
-def map_kernel(table, block_ref, place_ref, out_ref):
+def map_kernel(table, block_ref, place_ref, first_ref, second_ref):
     k = pl.program_id(0)
     live_row, live_col = table[16 + k], table[24 + k]
     target = lax.broadcasted_iota(I32, (BLK, BLK), 0)
@@ -399,30 +399,40 @@
     mapped = dot_nt(high, col_pick) + (dot_nt(middle, col_pick) + dot_nt(low, col_pick))
     opens = (k == 0) | (table[8 + k] != table[8 + jnp.maximum(k - 1, 0)])
 
-    @pl.when(opens)
-    def _():
-        out_ref[0] = mapped
-
-    @pl.when(jnp.logical_not(opens))
-    def _():
-        out_ref[0] = out_ref[0] + mapped
+    early = table[8 + k] < table[48]
+    for out_ref, mine in ((first_ref, early), (second_ref, jnp.logical_not(early))):
+
+        @pl.when(mine & opens)
+        def _():
+            out_ref[0] = mapped
+
+        @pl.when(mine & jnp.logical_not(opens))
+        def _():
+            out_ref[0] = out_ref[0] + mapped
 
 
 def map_children(child_blocks, child_target, child_place, child_live, mesh_cols):
     kids = child_blocks.shape[0]
     slot, _ = slots_of(child_target, mesh_cols)
     ordered = sort_order(slot)
+    spots = ordered(slot)
+    early = spots < mesh_cols
+    last = jnp.max(jnp.where(early, spots, 0))
+    opening = jnp.min(jnp.where(early, mesh_cols, spots - mesh_cols)) % mesh_cols
     table = jnp.concatenate(
         [
             ordered(jnp.arange(kids, dtype=I32)),
-            ordered(slot),
+            spots,
             ordered(child_live[:, 0]),
             ordered(child_live[:, 1]),
+            jnp.where(early, spots, last),
+            jnp.where(early, opening, spots - mesh_cols),
+            jnp.full((1,), mesh_cols, I32),
         ]
     )
     return pl.pallas_call(
         map_kernel,
-        out_shape=jax.ShapeDtypeStruct((mesh_cols * CAP, BLK, BLK), F32),
+        out_shape=[jax.ShapeDtypeStruct((mesh_cols, BLK, BLK), F32)] * CAP,
         grid_spec=pltpu.PrefetchScalarGridSpec(
             num_scalar_prefetch=1,
             grid=(kids,),
@@ -430,7 +440,10 @@
                 pl.BlockSpec((1, BLK, BLK), lambda k, t: (t[k], 0, 0)),
                 pl.BlockSpec((1, 2, BLK), lambda k, t: (t[k], 0, 0)),
             ],
-            out_specs=pl.BlockSpec((1, BLK, BLK), lambda k, t: (t[8 + k], 0, 0)),
+            out_specs=[
+                pl.BlockSpec((1, BLK, BLK), lambda k, t: (t[32 + k], 0, 0)),
+                pl.BlockSpec((1, BLK, BLK), lambda k, t: (t[40 + k], 0, 0)),
+            ],
         ),
         cost_estimate=pl.CostEstimate(flops=2_000_000_000, bytes_accessed=4 << 20, transcendentals=0),
         name="map_children",
@@ -600,14 +613,15 @@
     uc = col_pieces(late, core)
     share, four = lead_share(strip, core)
     raw = lax.all_gather(after(piece, four), "col", axis=0, tiled=False)
-    packed = map_children(child_blocks, child_target, child_place, child_live, mesh_cols)
+    first, second = map_children(child_blocks, child_target, child_place, child_live, mesh_cols)
 
     note = jnp.zeros((8, BLK), F32)
     note = note.at[0, : child_target.size].set(child_target.reshape(-1).astype(F32))
-    share = after(jnp.concatenate([share, note], axis=0), packed)
+    share, first, second = lax.optimization_barrier(
+        (jnp.concatenate([share, note], axis=0), first, second)
+    )
     uc = after(uc, four)
     own = to_all(share, "col")
-    first, second = packed[:mesh_cols], packed[mesh_cols:]
     first, uc = lax.optimization_barrier((first, uc, own))[:2]
     uc = ring_gather(uc, shift_z)
     first = exchange(first, "col")

time: 303 us -> 295 us (0.974)
  local copies, waits for them, and re-layouts: 19.9 us -> 12.9 us
  waiting for transfers between devices: 78.8 us -> 74.4 us
    ppermute x4, waiting for transfers between devices: 11.8 us -> 37.4 us  [col_pieces(): part = lax.ppermute(part, ('row', 'col'), pairs)]
    all_to_all x5, waiting for transfers between devices: 60.4 us -> 35 us  [exchange(): return lax.all_to_all(value, axis, split_axis=0, concat_axis=0, tiled=True)]
    all_to_all x5, starting transfers between devices: 35.3 us -> 47.3 us  [exchange(): return lax.all_to_all(value, axis, split_axis=0, concat_axis=0, tiled=True)]
    ppermute x2, starting transfers between devices: 11.1 us -> 0.09 us  [swap_cores(): return lax.ppermute(value, 'row', [(r, r ^ 1) for r in range(8)])]
    slice x1 -> x0, local copies, waits for them, and re-layouts: 7.71 us -> none  [on_device(): first, second = (packed[:mesh_cols], packed[mesh_cols:])]
    ppermute x3, waiting for transfers between devices: 6.53 us -> 0.01 us  [spread_x(): lax.ppermute(parts[q], 'col', [(y, q * SIDE + y) for y in range(SIDE)])]
  transfers between devices with their start and end apart: 18 -> 18, of which waited for: 7 -> 7; matrix products, arithmetic and copies ran while one was open for 7% -> 5% of each run, Pallas kernels for 36% -> 37%
where the time goes in v4:
time: 295 us; the launch traced here: 291 us
  Pallas kernels  118 us (40%)
  waiting for transfers between devices  74.4 us (25%)
  starting transfers between devices  59 us (20%)
  between operations  15.6 us (5%)
  local copies, waits for them, and re-layouts  12.9 us (4%)
  other arithmetic  11.7 us (4%)
    pallas_call x1, Pallas kernels, factor_lead(): pl.pallas_call(factor_kernel, out_shape=(jax.ShapeDtypeStruct((n, n), F32...  57.4 us
    all_to_all x5, starting transfers between devices, exchange(): return lax.all_to_all(value, axis, split_axis=0, concat_axis=0, tiled=True)  47.3 us
    ppermute x4, waiting for transfers between devices, col_pieces(): part = lax.ppermute(part, ('row', 'col'), pairs)  37.4 us
    pallas_call x1, Pallas kernels, update_front(): pl.pallas_call(update_kernel, out_shape=jax.ShapeDtypeStruct((rows, cols)...  36.1 us
    all_to_all x5, waiting for transfers between devices, exchange(): return lax.all_to_all(value, axis, split_axis=0, concat_axis=0, tiled=True)  35 us
    pallas_call x1, Pallas kernels, add_children(): pl.pallas_call(add_kernel, out_shape=jax.ShapeDtypeStruct(base.shape, F32...  10.2 us
    pallas_call x1, Pallas kernels, map_children(): pl.pallas_call(map_kernel, out_shape=[jax.ShapeDtypeStruct((mesh_cols, BL...  8.9 us
  transfers between devices with their start and end apart: 18, of which 7 were waited for; matrix products, arithmetic and copies ran while one was open for 5% of the time, Pallas kernels for 37%

profile of v4, /device:TPU:28, one launch (start us, length us, event | category | flops | bytes accessed | tf_op | source)
XLA Modules:
  0.0 291.1 jit_solution(4835463009949787666)
XLA Ops:
  6.5 1.7 slice.141
  8.2 7.1 %all-to-all-start = ((f32[16,16,256]{2,1,0:T(8,128)}), f32[16,16,256]{2,1,0:T(8,128)S(1)}, u32[]{:S(2)}, u32[]{:S(2)}) async-start(f32[16,16,256]{2,1,0:T(8,128)} %bitcast.1), calls=%async_computation | async-start | bytes 524288 | tf_op jit(solution)/shard_map/all_to_all | solution.py:62
  15.3 1.7 slice.157
  17.0 2.9 all-to-all-done
  19.9 1.2 fusion.10
  21.1 0.7 collective-permute-start.11
  21.8 1.3 collective-permute-start.10
  23.1 1.5 collective-permute-start.9
  24.6 0.9 broadcast_in_dim.30
  25.5 5.4 %all-to-all-start.1 = ((f32[8,4,16,256]{3,2,1,0:T(8,128)}), f32[8,4,16,256]{3,2,1,0:T(8,128)S(1)}, u32[]{:S(2)}, u32[]{:S(2)}) async-start(f32[8,4,16,256]{3,2,1,0:T(8,128)} %broadcast_in_dim.30), calls=%async_computation.1 | async-start | bytes 1048576 | tf_op jit(solution)/shard_map/all_to_all | solution.py:62
  31.0 10.3 %all-to-all-done.1 = f32[8,4,16,256]{3,2,1,0:T(8,128)S(1)} async-done(((f32[8,4,16,256]{3,2,1,0:T(8,128)}), f32[8,4,16,256]{3,2,1,0:T(8,128)S(1)}, u32[]{:S(2)}, u32[]{:S(2)}) %all-to-all-start.1) | async-done | bytes 524320 | tf_op jit(solution)/shard_map/all_to_all | solution.py:62
  41.3 2.1 add_add_fusion
  43.7 0.2 convert_reduce_fusion.1
  43.9 0.2 convert_reduce_fusion
  44.3 0.7 fusion.6
  47.0 0.6 compare_select_fusion.6
  47.7 0.7 concatenate.23.table
  48.3 8.9 %map_children.1 = (f32[16,256,256]{2,1,0:T(8,128)}, f32[16,256,256]{2,1,0:T(8,128)}) custom-call(s32[49]{0:T(128)} %concatenate.23.table, f32[8,256,256]{2,1,0:T(8,128)} %block_ref.1, s32[8,2,256]{2,1,0:T(2,128)} %place_ref.1), custom_call_target="tpu_custom_call" | custom-call | flops 2000000000 | bytes 4194304 | tf_op jit(solution)/shard_map/map_children/pallas_call | solution.py:433
  57.3 1.2 broadcast_in_dim.38
  58.6 14.4 %all-to-all-start.2 = ((f32[16,88,256]{2,1,0:T(8,128)}), f32[16,88,256]{2,1,0:T(8,128)S(1)}, u32[]{:S(2)}, u32[]{:S(2)}) async-start(f32[16,88,256]{2,1,0:T(8,128)} %broadcast_in_dim.38), calls=%async_computation.2 | async-start | bytes 2883584 | tf_op jit(solution)/shard_map/all_to_all | solution.py:62
  73.1 0.8 pad_maximum_fusion.4
  74.0 0.7 collective-permute-start.4
  74.6 0.8 pad_maximum_fusion.3
  75.5 1.3 collective-permute-start.3
  76.8 0.8 pad_maximum_fusion.1
  77.6 1.5 collective-permute-start.1
  79.1 0.8 pad_maximum_fusion.2
  79.9 1.5 collective-permute-start.2
  81.3 10.6 %all-to-all-done.2.own_ref = f32[16,88,256]{2,1,0:T(8,128)S(1)} async-done(((f32[16,88,256]{2,1,0:T(8,128)}), f32[16,88,256]{2,1,0:T(8,128)S(1)}, u32[]{:S(2)}, u32[]{:S(2)}) %all-to-all-start.2) | async-done | bytes 1441824 | tf_op jit(solution)/shard_map/all_to_all | solution.py:62
  92.0 37.4 %collective-permute-done.3 = f32[2,256,256]{2,1,0:T(8,128)} collective-permute-done((f32[2,256,256]{2,1,0:T(8,128)}, f32[2,256,256]{2,1,0:T(8,128)}, u32[]{:S(2)}, u32[]{:S(2)}) %collective-permute-start.3) | collective-permute-done | bytes 524320 | tf_op jit(solution)/shard_map/ppermute | solution.py:89
  129.4 1.7 add_add_fusion.1
  131.2 1.9 collective-permute-done.5
  133.2 1.1 pad_maximum_fusion.refs_0_
  134.3 3.2 %collective-permute-start.7 = (f32[4,256,256]{2,1,0:T(8,128)}, f32[4,256,256]{2,1,0:T(8,128)}, u32[]{:S(2)}, u32[]{:S(2)}) collective-permute-start(f32[4,256,256]{2,1,0:T(8,128)} %pad_maximum_fusion.refs_0_), channel_id=1, source_target_pairs={{0,96},{16,112},{32,0},{48,16},{64,32},{80,48},{96,64},{112,80},{1... | collective-permute-start | bytes 3145736 | tf_op jit(solution)/shard_map/ppermute | solution.py:39
  137.5 13.4 %all-to-all-start.3 = ((f32[16,256,256]{2,1,0:T(8,128)}), f32[16,256,256]{2,1,0:T(8,128)}, u32[]{:S(2)}, u32[]{:S(2)}) async-start(f32[16,256,256]{2,1,0:T(8,128)} %get-tuple-element.53), calls=%async_computation.3 | async-start | bytes 8388608 | tf_op jit(solution)/shard_map/all_to_all | solution.py:62
  150.9 57.4 %factor_lead.1 = (f32[1024,1024]{1,0:T(8,128)S(1)}, bf16[1024,1024]{1,0:T(8,128)(2,1)S(1)}, bf16[1024,1024]{1,0:T(8,128)(2,1)S(1)}) custom-call(s32[1]{0:T(128)} %bitcast.18.table, f32[16,88,256]{2,1,0:T(8,128)S(1)} %all-to-all-done.2.own_ref, f32[16,88,256]{2,1,0:T(8,128)S(1)} %collective-permute-done.other_ref), custom_call_target="tpu_custom_call" | custom-call | flops 60000002048 | bytes 10485760 | tf_op jit(solution)/shard_map/factor_lead/pallas_call | solution.py:219
  208.4 2.0 copy-done.1
  210.3 1.4 copy-done.2
  211.7 1.3 copy-done.3
  213.1 3.7 %all-to-all-done.3.first_ref = f32[16,256,256]{2,1,0:T(8,128)} async-done(((f32[16,256,256]{2,1,0:T(8,128)}), f32[16,256,256]{2,1,0:T(8,128)}, u32[]{:S(2)}, u32[]{:S(2)}) %all-to-all-start.3) | async-done | bytes 4194336 | tf_op jit(solution)/shard_map/all_to_all | solution.py:62
  216.7 6.9 %all-to-all-start.4 = ((f32[16,256,256]{2,1,0:T(8,128)}), f32[16,256,256]{2,1,0:T(8,128)}, u32[]{:S(2)}, u32[]{:S(2)}) async-start(f32[16,256,256]{2,1,0:T(8,128)} %get-tuple-element.54), calls=%async_computation.4 | async-start | bytes 8388608 | tf_op jit(solution)/shard_map/all_to_all | solution.py:62
  223.7 0.7 pad_add_fusion.table
  224.3 0.5 copy.23
  224.8 0.6 fusion.notes_ref
  225.4 4.9 %add_table.1.table = s32[65]{0:T(128)} custom-call(s32[1]{0:T(128)} %bitcast.info_ref, s32[16,16]{1,0:T(8,128)} %fusion.notes_ref), custom_call_target="tpu_custom_call" | custom-call | tf_op jit(solution)/shard_map/add_table/pallas_call | solution.py:560
  230.4 36.1 %update_front.1.base_ref = f32[2048,1024]{1,0:T(8,128)} custom-call(s32[6]{0:T(128)} %pad_add_fusion.table, f32[4,256,256]{2,1,0:T(8,128)} %pad_maximum_fusion.refs_0_, f32[4,256,256]{2,1,0:T(8,128)} %collective-permute-done.6.refs_1_, f32[4,256,256]{2,1,0:T(8,128)} %collective-permute-done.7.refs_2_, f32[4,256,256]{2,1,0:T(8,128)} %collective-permute-done.8.refs_3_, ...), custom_call_target="tpu_custom_call" | custom-call | flops 25999998976 | bytes 37748736 | tf_op jit(solution)/shard_map/update_front/pallas_call | solution.py:334
  266.5 7.5 %all-to-all-done.4.second_ref = f32[16,256,256]{2,1,0:T(8,128)} async-done(((f32[16,256,256]{2,1,0:T(8,128)}), f32[16,256,256]{2,1,0:T(8,128)}, u32[]{:S(2)}, u32[]{:S(2)}) %all-to-all-start.4) | async-done | bytes 4194336 | tf_op jit(solution)/shard_map/all_to_all | solution.py:62
  274.0 10.2 %add_children.1 = f32[2048,1024]{1,0:T(8,128)} custom-call(s32[65]{0:T(128)S(1)} %copy-done, f32[2048,1024]{1,0:T(8,128)} %update_front.1.base_ref, f32[16,256,256]{2,1,0:T(8,128)} %all-to-all-done.3.first_ref, f32[16,256,256]{2,1,0:T(8,128)} %all-to-all-done.4.second_ref), custom_call_target="tpu_custom_call", output_to_operand_aliasing={{}: (1, {})} | custom-call | flops 4000000 | bytes 25165824 | tf_op jit(solution)/shard_map/add_children/pallas_call | solution.py:577
  (53 shorter events, 1.1 us)
Async XLA Ops:
  8.2 11.7 %all-to-all-start = ((f32[16,16,256]{2,1,0:T(8,128)}), f32[16,16,256]{2,1,0:T(8,128)S(1)}, u32[]{:S(2)}, u32[]{:S(2)}) async-start(f32[16,16,256]{2,1,0:T(8,128)} %bitcast.1), calls=%async_computation | async-start | bytes 524288 | tf_op jit(solution)/shard_map/all_to_all | solution.py:62
  21.1 20.1 %collective-permute-start.11 = (f32[512,256]{1,0:T(8,128)}, f32[512,256]{1,0:T(8,128)S(1)}, u32[]{:S(2)}, u32[]{:S(2)}) collective-permute-start(f32[512,256]{1,0:T(8,128)} %get-tuple-element.62), channel_id=1, source_target_pairs={{0,12},{1,13},{2,14},{3,15},{16,28},{17,29},{18,30},{19,31},{32,44... | collective-permute-start | bytes 1572872 | tf_op jit(solution)/shard_map/ppermute | solution.py:53
  21.8 19.4 %collective-permute-start.10 = (f32[512,256]{1,0:T(8,128)}, f32[512,256]{1,0:T(8,128)}, u32[]{:S(2)}, u32[]{:S(2)}) collective-permute-start(f32[512,256]{1,0:T(8,128)} %get-tuple-element.63), channel_id=1, source_target_pairs={{0,8},{1,9},{2,10},{3,11},{16,24},{17,25},{18,26},{19,27},{32,40},... | collective-permute-start | bytes 1572872 | tf_op jit(solution)/shard_map/ppermute | solution.py:53
  23.1 18.1 %collective-permute-start.9 = (f32[512,256]{1,0:T(8,128)}, f32[512,256]{1,0:T(8,128)}, u32[]{:S(2)}, u32[]{:S(2)}) collective-permute-start(f32[512,256]{1,0:T(8,128)} %get-tuple-element.61), channel_id=1, source_target_pairs={{0,4},{1,5},{2,6},{3,7},{16,20},{17,21},{18,22},{19,23},{32,36},{3... | collective-permute-start | bytes 1572872 | tf_op jit(solution)/shard_map/ppermute | solution.py:53
  25.5 18.0 %copy-start.5 = (s32[8,2]{0,1:T(2,128)S(1)}, s32[8,2]{0,1:T(2,128)}, u32[]{:S(2)}) copy-start(s32[8,2]{0,1:T(2,128)} %param.10) | copy-start | bytes 196
  25.5 18.6 %copy-start.6 = (s32[8,2]{0,1:T(2,128)S(1)}, s32[8,2]{0,1:T(2,128)}, u32[]{:S(2)}) copy-start(s32[8,2]{0,1:T(2,128)} %param.12) | copy-start | bytes 196
  25.5 15.8 %all-to-all-start.1 = ((f32[8,4,16,256]{3,2,1,0:T(8,128)}), f32[8,4,16,256]{3,2,1,0:T(8,128)S(1)}, u32[]{:S(2)}, u32[]{:S(2)}) async-start(f32[8,4,16,256]{3,2,1,0:T(8,128)} %broadcast_in_dim.30), calls=%async_computation.1 | async-start | bytes 1048576 | tf_op jit(solution)/shard_map/all_to_all | solution.py:62
  30.9 199.4 %all-gather.3.cloned.1.call-start = ((), (), s32[]{:S(2)}) async-start(), calls=%async_computation.5 | async-start | bytes 8912896 | tf_op jit(solution)/shard_map/all_gather | solution.py:615
  58.6 33.4 %all-to-all-start.2 = ((f32[16,88,256]{2,1,0:T(8,128)}), f32[16,88,256]{2,1,0:T(8,128)S(1)}, u32[]{:S(2)}, u32[]{:S(2)}) async-start(f32[16,88,256]{2,1,0:T(8,128)} %broadcast_in_dim.38), calls=%async_computation.2 | async-start | bytes 2883584 | tf_op jit(solution)/shard_map/all_to_all | solution.py:62
  74.0 18.0 %collective-permute-start.4 = (f32[2,256,256]{2,1,0:T(8,128)}, f32[2,256,256]{2,1,0:T(8,128)S(1)}, u32[]{:S(2)}, u32[]{:S(2)}) collective-permute-start(f32[2,256,256]{2,1,0:T(8,128)} %pad_maximum_fusion.4), channel_id=1, source_target_pairs={{0,24},{1,56},{2,88},{3,120},{16,25},{17,57},{18,89},{19,121},{32,... | collective-permute-start | bytes 1572872 | tf_op jit(solution)/shard_map/ppermute | solution.py:89
  75.5 53.9 %collective-permute-start.3 = (f32[2,256,256]{2,1,0:T(8,128)}, f32[2,256,256]{2,1,0:T(8,128)}, u32[]{:S(2)}, u32[]{:S(2)}) collective-permute-start(f32[2,256,256]{2,1,0:T(8,128)} %pad_maximum_fusion.3), channel_id=1, source_target_pairs={{0,8},{1,40},{2,72},{3,104},{16,9},{17,41},{18,73},{19,105},{32,10... | collective-permute-start | bytes 1572872 | tf_op jit(solution)/shard_map/ppermute | solution.py:89
  77.6 51.8 %collective-permute-start.1 = (f32[2,256,256]{2,1,0:T(8,128)}, f32[2,256,256]{2,1,0:T(8,128)}, u32[]{:S(2)}, u32[]{:S(2)}) collective-permute-start(f32[2,256,256]{2,1,0:T(8,128)} %pad_maximum_fusion.1), channel_id=1, source_target_pairs={{0,0},{1,32},{2,64},{3,96},{16,1},{17,33},{18,65},{19,97},{32,2},{... | collective-permute-start | bytes 1572872 | tf_op jit(solution)/shard_map/ppermute | solution.py:89
  79.9 49.5 %collective-permute-start.2 = (f32[2,256,256]{2,1,0:T(8,128)}, f32[2,256,256]{2,1,0:T(8,128)}, u32[]{:S(2)}, u32[]{:S(2)}) collective-permute-start(f32[2,256,256]{2,1,0:T(8,128)} %pad_maximum_fusion.2), channel_id=1, source_target_pairs={{0,16},{1,48},{2,80},{3,112},{16,17},{17,49},{18,81},{19,113},{32,... | collective-permute-start | bytes 1572872 | tf_op jit(solution)/shard_map/ppermute | solution.py:89
  92.0 58.9 %collective-permute-start = (f32[16,88,256]{2,1,0:T(8,128)S(1)}, f32[16,88,256]{2,1,0:T(8,128)S(1)}, u32[]{:S(2)}, u32[]{:S(2)}) collective-permute-start(f32[16,88,256]{2,1,0:T(8,128)S(1)} %all-to-all-done.2.own_ref), channel_id=1, source_target_pairs={{0,16},{16,0},{32,48},{48,32},{64,80},{80,64},{96,112},{112,96},{1... | collective-permute-start | bytes 4325384 | tf_op jit(solution)/shard_map/ppermute | solution.py:43
  92.0 37.4 %copy-start.4 = (f32[2,256,256]{2,1,0:T(8,128)}, f32[2,256,256]{2,1,0:T(8,128)S(1)}, u32[]{:S(2)}) copy-start(f32[2,256,256]{2,1,0:T(8,128)S(1)} %collective-permute-done.4) | copy-start | bytes 1572868
  131.1 2.0 collective-permute-start.5
  134.3 78.7 %collective-permute-start.6 = (f32[4,256,256]{2,1,0:T(8,128)}, f32[4,256,256]{2,1,0:T(8,128)}, u32[]{:S(2)}, u32[]{:S(2)}) collective-permute-start(f32[4,256,256]{2,1,0:T(8,128)} %pad_maximum_fusion.refs_0_), channel_id=1, source_target_pairs={{0,32},{16,48},{32,64},{48,80},{64,96},{80,112},{96,0},{112,16},{1... | collective-permute-start | bytes 3145736 | tf_op jit(solution)/shard_map/ppermute | solution.py:39
  134.3 78.7 %collective-permute-start.7 = (f32[4,256,256]{2,1,0:T(8,128)}, f32[4,256,256]{2,1,0:T(8,128)}, u32[]{:S(2)}, u32[]{:S(2)}) collective-permute-start(f32[4,256,256]{2,1,0:T(8,128)} %pad_maximum_fusion.refs_0_), channel_id=1, source_target_pairs={{0,96},{16,112},{32,0},{48,16},{64,32},{80,48},{96,64},{112,80},{1... | collective-permute-start | bytes 3145736 | tf_op jit(solution)/shard_map/ppermute | solution.py:39
  137.5 75.5 %collective-permute-start.8 = (f32[4,256,256]{2,1,0:T(8,128)}, f32[4,256,256]{2,1,0:T(8,128)}, u32[]{:S(2)}, u32[]{:S(2)}) collective-permute-start(f32[4,256,256]{2,1,0:T(8,128)} %pad_maximum_fusion.refs_0_), channel_id=1, source_target_pairs={{0,64},{16,80},{32,96},{48,112},{64,0},{80,16},{96,32},{112,48},{1... | collective-permute-start | bytes 3145736 | tf_op jit(solution)/shard_map/ppermute | solution.py:39
  137.5 79.2 %all-to-all-start.3 = ((f32[16,256,256]{2,1,0:T(8,128)}), f32[16,256,256]{2,1,0:T(8,128)}, u32[]{:S(2)}, u32[]{:S(2)}) async-start(f32[16,256,256]{2,1,0:T(8,128)} %get-tuple-element.53), calls=%async_computation.3 | async-start | bytes 8388608 | tf_op jit(solution)/shard_map/all_to_all | solution.py:62
  208.3 2.0 copy-start.1
  210.3 1.4 copy-start.2
  211.7 1.3 copy-start.3
  213.0 10.6 %copy-start.7 = (s32[4]{0:T(128)S(1)}, s32[4]{0:T(128)}, u32[]{:S(2)}) copy-start(s32[4]{0:T(128)} %constant.123.clone) | copy-start | bytes 52
  216.7 57.3 %all-to-all-start.4 = ((f32[16,256,256]{2,1,0:T(8,128)}), f32[16,256,256]{2,1,0:T(8,128)}, u32[]{:S(2)}, u32[]{:S(2)}) async-start(f32[16,256,256]{2,1,0:T(8,128)} %get-tuple-element.54), calls=%async_computation.4 | async-start | bytes 8388608 | tf_op jit(solution)/shard_map/all_to_all | solution.py:62
  230.4 43.7 %copy-start = (s32[65]{0:T(128)S(1)}, s32[65]{0:T(128)}, u32[]{:S(2)}) copy-start(s32[65]{0:T(128)} %add_table.1.table) | copy-start | bytes 784
Sparse Core Ops, SparseCore 0:
  43.5 103.8 all-gather.2
